TPU v7x, 32 devices: a whole 2x2x4 slice. The times are simulated.
32 devices in a mesh: section: 4 (over x, core), dp: 8 (over z, y).
Axes of the slice: x: 2, y: 2, z: 4, core: 2. Of those that a mesh axis runs over, the one named last changes fastest.
Arguments:
- global_rows: bfloat16 [16, 2, 197, 384], P('dp'), may hold values from -6 to 6
- local_rows: bfloat16 [16, 10, 37, 384], P('dp'), may hold values from -6 to 6
- patch_rank: int32 [16, 2, 196], P('dp'), may hold values from 0 to 195, as said below
- ratio_bin: int32 [16], P('dp'), may hold values from 0 to 4
- mask_token: bfloat16 [1, 384], replicated, may hold values from -4 to 4
- attend_gain: bfloat16 [2, 384], replicated, may hold values from 0.099609375 to 1.8984375
- attend_shift: bfloat16 [2, 384], replicated, may hold values from -2 to 2
- triple_weight: bfloat16 [2, 384, 1152], replicated, may hold values from -0.3125 to 0.3125
- pair_bias: bfloat16 [2, 768], replicated, may hold values from -3 to 3
- output_weight: bfloat16 [2, 384, 384], replicated, may hold values from -2.5 to 2.5
- output_bias: bfloat16 [2, 384], replicated, may hold values from -2 to 2
- expand_gain: bfloat16 [2, 384], replicated, may hold values from 0.099609375 to 1.8984375
- expand_shift: bfloat16 [2, 384], replicated, may hold values from -2 to 2
- up_weight: bfloat16 [2, 384, 1536], replicated, may hold values from -0.3125 to 0.3125
- up_bias: bfloat16 [2, 1536], replicated, may hold values from -3 to 3
- down_weight: bfloat16 [2, 1536, 384], replicated, may hold values from -0.15625 to 0.15625
- down_bias: bfloat16 [2, 384], replicated, may hold values from -2 to 2
- grad_global: bfloat16 [16, 2, 197, 384], P('dp'), may hold values from -6 to 6
- grad_local: bfloat16 [16, 10, 37, 384], P('dp'), may hold values from -6 to 6
Outputs:
- out_global: float32 [16, 2, 197, 384], P('dp', None, None, 'section')
- out_local: float32 [16, 10, 37, 384], P('dp', None, None, 'section')
- input_grad_global: float32 [16, 2, 197, 384], P('dp', None, None, 'section')
- input_grad_local: float32 [16, 10, 37, 384], P('dp', None, None, 'section')
- token_grad: float32 [1, 384], P(None, 'section')
- attend_gain_grad: float32 [2, 384], P(None, 'section')
- attend_shift_grad: float32 [2, 384], P(None, 'section')
- triple_weight_grad: float32 [2, 384, 1152], P(None, 'section')
- pair_bias_grad: float32 [2, 768], P(None, 'section')
- output_weight_grad: float32 [2, 384, 384], P(None, 'section')
- output_bias_grad: float32 [2, 384], P(None, 'section')
- expand_gain_grad: float32 [2, 384], P(None, 'section')
- expand_shift_grad: float32 [2, 384], P(None, 'section')
- up_weight_grad: float32 [2, 384, 1536], P(None, 'section')
- up_bias_grad: float32 [2, 1536], P(None, 'section')
- down_weight_grad: float32 [2, 1536, 384], P(None, 'section')
- down_bias_grad: float32 [2, 384], P(None, 'section')
Inputs may be any that keep to these rules, and one draw needn't show every extreme that they name: In each global crop, patch_rank holds every number from 0 to 195 once; the four patches of each aligned 2 x 2 square of the crop's 14 x 14 grid of patches (row-major) hold four consecutive ranks that start at a multiple of 4.
All inputs are finite; a program needn't handle non-finite values.
Results may differ from a plain program's by a relative error of at most 0.015.
Values may be sent and summed in bfloat16 or wider, within the bound.
No kernel may reach another device: no remote copies, remote signals or barrier semaphores. Data moves between devices by JAX's collectives and lax.ppermute only.
A program may use at most 320 MiB of HBM per device.

v0:
```python
import math

import jax
import jax.numpy as jnp
from jax import lax
from jax.experimental import pallas as pl
from jax.experimental.pallas import tpu as pltpu
from jax.sharding import PartitionSpec as P

HEADS = 6
EPS = 1e-06
LANES = 128
VMEM_MIB = {"front": 26, "finish": 20}
CHOICES = (0, 0, 1, 0)
PLAN = (
    "A later_core later_attend A expand core",
    "C B A C B attend",
    "D C D A B output R",
    "A B D C B A C D B",
    "A D C R B D C R D A",
    "C B D A B R early C D",
)
X_AXIS = -1

f32 = jnp.float32
bf16 = jnp.bfloat16


def up_to(value, step):
    return (value + step - 1) // step * step


class Sizes:
    def __init__(self, global_rows, local_rows, up_weight, sections, replicas):
        images, crops, self.global_len, self.width = global_rows.shape
        _, local_crops, self.local_len, _ = local_rows.shape
        self.hidden = up_weight.shape[2]
        self.sections = sections
        self.replicas = replicas
        self.images = images
        self.all_globals = images * crops
        self.all_locals = images * local_crops
        self.locals = self.all_locals // sections
        self.used = self.global_len + self.locals * self.local_len
        self.rows = up_to(self.used, LANES)
        self.head = self.width // HEADS
        self.cut = self.width // sections
        self.hidden_cut = self.hidden // sections
        self.tiles = self.width // LANES
        self.first_end = up_to(self.global_len, 16)
        self.second_start = self.global_len // 16 * 16
        self.windows = (
            (0, self.first_end),
            (self.second_start, self.rows - self.second_start),
        )
        self.attend_full = 4 * self.tiles * self.cut
        self.expand_full = self.hidden // LANES * self.cut + self.tiles * self.hidden_cut
        self.small_rows = up_to(max(6 * self.tiles, 3 * self.tiles + self.hidden // LANES), 16)
        self.extra = self.cut * self.rows // LANES
        bits = replicas.bit_length() - 1
        low = list(range(min(bits, 2)))
        last_first = low[1:] + [X_AXIS] + low[:1]
        first_last = [X_AXIS] + low
        middle = low[:1] + [X_AXIS] + low[1:]
        choices = (
            (first_last, last_first), (middle, last_first), (first_last, middle), ([X_AXIS] + low[1:], low[1:] + [X_AXIS])
        )
        self.exchanges = {name: Exchange(choices[choice], bits) for name, choice in zip("ABCD", CHOICES)}
        self.unit = 16 << len(low)

    def packed(self, full):
        return up_to(full + self.small_rows, self.unit)


class Exchange:
    def __init__(self, orders, bits):
        self.orders = orders
        self.axes = sorted(axis for axis in orders[0] if axis != X_AXIS)
        self.rest = [axis for axis in range(bits) if axis not in self.axes]
        self.shards = 1 << len(self.axes)

    def shard_of(self, replica):
        return sum((replica >> axis & 1) << i for i, axis in enumerate(self.axes))

    def place(self, core, across, offset):
        order = self.orders[core]
        return sum(
            (across if axis == X_AXIS else offset >> self.axes.index(axis) & 1) << (len(order) - 1 - at)
            for at, axis in enumerate(order)
        )

    def offset(self, core, place):
        order = [axis for axis in self.orders[core] if axis != X_AXIS]
        return sum((place >> (len(order) - 1 - at) & 1) << self.axes.index(axis) for at, axis in enumerate(order))


def dot(a, b):
    return jnp.dot(a, b, preferred_element_type=f32)


def dot_last(a, b):
    return lax.dot_general(a, b, (((1,), (1,)), ((), ())), preferred_element_type=f32)


def dot_first(a, b):
    return lax.dot_general(a, b, (((0,), (0,)), ((), ())), preferred_element_type=f32)


def normalize(hidden):
    average = jnp.mean(hidden, axis=-1, keepdims=True)
    centred = hidden - average
    inverse = lax.rsqrt(jnp.mean(centred * centred, axis=-1, keepdims=True) + EPS)
    return centred * inverse, inverse


def row_blocks(sz):
    return [slice(i, i + LANES) for i in range(0, sz.rows, LANES)]


def head_mask(sz, rows, which):
    lane = lax.broadcasted_iota(jnp.int32, (rows, 2 * sz.head), 1)
    return lane < sz.head if which == 0 else lane >= sz.head


def window_bias(sz, which):
    start, length = sz.windows[which]

    def group(row):
        if which == 0:
            return jnp.where(row < sz.global_len, 0, 1)
        kind = jnp.where(row + start < sz.global_len, 0, 1)
        for crop in range(1, sz.locals + 1):
            kind = kind + jnp.where(row + start >= sz.global_len + crop * sz.local_len, 1, 0)
        return kind

    left = group(lax.broadcasted_iota(jnp.int32, (length, length), 0))
    right = group(lax.broadcasted_iota(jnp.int32, (length, length), 1))
    return jnp.where(left == right, 0.0, -1e30).astype(f32)


def own_rows(sz, which):
    start, length = sz.windows[which]
    row = lax.broadcasted_iota(jnp.int32, (length, 1), 0) + start
    return row < sz.global_len if which == 0 else row >= sz.global_len


def store_window(sz, which, ref, columns, value):
    start, length = sz.windows[which]
    if which == 0 or sz.first_end == start:
        ref[start : start + length, columns] = value.astype(bf16)
        return
    shared = sz.first_end - start
    row = lax.broadcasted_iota(jnp.int32, (shared, value.shape[1]), 0) + start
    before = ref[start : sz.first_end, columns].astype(f32)
    ref[start : sz.first_end, columns] = jnp.where(
        row < sz.global_len, before, value[:shared]
    ).astype(bf16)
    ref[sz.first_end : start + length, columns] = value[shared:].astype(bf16)


def norm_rows(sz, h_ref, gain, shift, normed_ref):
    for rows in row_blocks(sz):
        scaled, _ = normalize(h_ref[rows, :].astype(f32))
        normed_ref[rows, :] = (scaled * gain + shift).astype(bf16)


def stacked_heads(sz, value):
    zero = jnp.zeros_like(value)
    return jnp.concatenate([jnp.where(head_mask(sz, value.shape[0], which), value, zero) for which in range(2)], axis=0)


def attend_forward(sz, h_ref, weights, out_ref, normed_ref, qkv_ref, lse_ref, ctx_ref, bias_refs):
    gain, shift, triple_ref, pair_bias, output_ref, output_bias = weights
    width = sz.width
    norm_rows(sz, h_ref, gain, shift, normed_ref)
    scale = 1.0 / math.sqrt(sz.head)
    for part in range(3):
        columns = slice(part * width, (part + 1) * width)
        project = dot(normed_ref[...], triple_ref[:, columns])
        if part == 0:
            project = (project + pair_bias[:, :width]) * scale
        if part == 2:
            project = project + pair_bias[:, width:]
        qkv_ref[:, columns] = project.astype(bf16)
    for which, (start, length) in enumerate(sz.windows):
        rows = slice(start, start + length)
        bias = bias_refs[which]
        lane = lax.broadcasted_iota(jnp.int32, (length, LANES), 1)
        first = head_mask(sz, length, 0)
        kept = jnp.zeros((length, LANES), f32)
        for pair in range(HEADS // 2):
            at = 2 * sz.head * pair
            queries, keys, values = (
                qkv_ref[rows, part * width + at : part * width + at + 2 * sz.head] for part in range(3)
            )
            scores = dot_last(stacked_heads(sz, queries), keys)
            probs = []
            for which_head in range(2):
                own = scores[which_head * length : (which_head + 1) * length] + bias[...]
                top = jnp.max(own, axis=-1, keepdims=True)
                raised = jnp.exp(own - top)
                total = jnp.sum(raised, axis=-1, keepdims=True)
                kept = jnp.where(lane == 2 * pair + which_head, top + jnp.log(total), kept)
                probs.append((raised * (1.0 / total)).astype(bf16))
            context = dot(jnp.concatenate(probs, axis=0), values)
            store_window(
                sz, which, ctx_ref, slice(at, at + 2 * sz.head), jnp.where(first, context[:length], context[length:])
            )
        lse_ref[8 * which : 8 * which + 8, :length] = kept.T[:8]
    moved = dot(ctx_ref[...], output_ref[...]) + output_bias
    out_ref[...] = (h_ref[...].astype(f32) + moved).astype(bf16)


def expand_hidden(sz, h_ref, weights, normed_ref, active_ref, slope_ref):
    gain, shift, up_ref, up_bias = weights
    norm_rows(sz, h_ref, gain, shift, normed_ref)
    for at in range(0, sz.hidden, sz.hidden_cut):
        columns = slice(at, at + sz.hidden_cut)
        before = dot(normed_ref[...], up_ref[:, columns]) + up_bias[:, columns]
        share = 0.5 + 0.5 * lax.erf(before * math.sqrt(0.5))
        active_ref[:, columns] = (before * share).astype(bf16)
        density = jnp.exp(before * before * -0.5) * (1.0 / math.sqrt(2.0 * math.pi))
        slope_ref[:, columns] = (share + before * density).astype(bf16)


def expand_output(h_ref, active_ref, down_ref, down_bias):
    return h_ref[...].astype(f32) + dot(active_ref[...], down_ref[...]) + down_bias


def turned_blocks(sz, value, me, turned_ref, blocks_ref):
    turned_ref[...] = value.T
    for j in range(sz.sections):
        source = pl.multiple_of((me ^ j) * sz.cut, sz.cut)
        blocks_ref[j * sz.cut : (j + 1) * sz.cut, :] = turned_ref[pl.ds(source, sz.cut), :]


def put_vector(small, at, vector):
    for tile in range(vector.shape[1] // LANES):
        small[at + tile : at + tile + 1, :] = vector[:, tile * LANES : (tile + 1) * LANES]
    return at + vector.shape[1] // LANES


def put_tiles(pack, j, at, value):
    r = value.shape[0]
    for tile in range(value.shape[1] // LANES):
        pack[j, pl.ds(at + tile * r, r), :] = value[:, tile * LANES : (tile + 1) * LANES].astype(bf16)


def norm_backward(sz, h_ref, grad_ref, grad_normed_ref, gain, dh_ref):
    gain_sum = jnp.zeros((1, sz.width), f32)
    shift_sum = jnp.zeros((1, sz.width), f32)
    for rows in row_blocks(sz):
        scaled, inverse = normalize(h_ref[rows, :].astype(f32))
        grad_normed = grad_normed_ref[rows, :]
        grad_scaled = grad_normed * gain
        first = jnp.mean(grad_scaled, axis=-1, keepdims=True)
        second = jnp.mean(grad_scaled * scaled, axis=-1, keepdims=True)
        grad_in = inverse * (grad_scaled - first - scaled * second)
        dh_ref[rows, :] = (grad_ref[rows, :].astype(f32) + grad_in).astype(dh_ref.dtype)
        gain_sum += jnp.sum(grad_normed * scaled, axis=0, keepdims=True)
        shift_sum += jnp.sum(grad_normed, axis=0, keepdims=True)
    return gain_sum, shift_sum


def expand_backward(sz, me, h_ref, normed, grad_ref, act_ref, slope_ref, gain, up, down, dh_ref, scratch, pack, small):
    total, turned, blocks = scratch
    base = 0
    part = sz.hidden_cut
    up_rows = sz.hidden // LANES * sz.cut
    turned_blocks(sz, normed[...], me, turned, blocks)
    after = 2 * sz.tiles
    for j in range(sz.sections):
        owner = me ^ j
        columns = pl.ds(pl.multiple_of(owner * part, LANES), part)
        put_tiles(pack, j, base + up_rows, dot_first(act_ref[:, columns], grad_ref[...]))
        grad_active = dot_last(grad_ref[...], down[columns, :])
        grad_before = (grad_active * slope_ref[:, columns].astype(f32)).astype(bf16)
        up_sum = jnp.sum(grad_before.astype(f32), axis=0, keepdims=True)
        for tile in range(part // LANES):
            small[pl.ds(after + owner * (part // LANES) + tile, 1), :] = up_sum[:, tile * LANES : (tile + 1) * LANES]
        up_grad = dot(blocks[...], grad_before)
        at = base + pl.multiple_of(owner * (part // LANES * sz.cut), 16)
        for other in range(sz.sections):
            put_tiles(pack, other, at, up_grad[other * sz.cut : (other + 1) * sz.cut, :])
        more = dot_last(grad_before, up[:, columns])
        if j == 0:
            total[...] = more
        else:
            total[...] += more
    gain_sum, shift_sum = norm_backward(sz, h_ref, grad_ref, total, gain, dh_ref)
    put_vector(small, 0, gain_sum)
    put_vector(small, sz.tiles, shift_sum)
    put_vector(
        small, after + sz.hidden // LANES, jnp.sum(grad_ref[...].astype(f32), axis=0, keepdims=True)
    )


def attend_core_backward(sz, grad_ref, output, qkv_ref, lse_ref, proj, dctx, bias_refs):
    width = sz.width
    dctx[...] = dot_last(grad_ref[...], output[...]).astype(bf16)
    scale = 1.0 / math.sqrt(sz.head)
    for which, (start, length) in enumerate(sz.windows):
        rows = slice(start, start + length)
        bias = bias_refs[which]
        own = own_rows(sz, which)
        for pair in range(HEADS // 2):
            at = 2 * sz.head * pair
            columns = [slice(part * width + at, part * width + at + 2 * sz.head) for part in range(3)]
            queries, keys, values = (qkv_ref[rows, c] for c in columns)
            grad_ctx = jnp.where(own, dctx[rows, columns[0]], jnp.zeros((length, 2 * sz.head), bf16))
            keys = stacked_heads(sz, keys)
            scores = dot_last(keys, queries)
            grad_probs = dot_last(stacked_heads(sz, values), grad_ctx)
            probs, grad_scores = [], []
            for which_head in range(2):
                part = slice(which_head * length, (which_head + 1) * length)
                row = 8 * which + 2 * pair + which_head
                prob = jnp.exp(scores[part] + bias[...] - lse_ref[row : row + 1, :length])
                grad_prob = grad_probs[part]
                delta = jnp.sum(prob * grad_prob, axis=0, keepdims=True)
                grad_scores.append((prob * (grad_prob - delta)).astype(bf16))
                probs.append(prob.astype(bf16))
            grad_scores = jnp.concatenate(grad_scores, axis=0)
            first = head_mask(sz, length, 0)
            grad_keys = dot(grad_scores, queries)
            grad_values = dot(jnp.concatenate(probs, axis=0), grad_ctx)
            store_window(sz, which, proj, columns[0], dot_first(grad_scores, keys) * scale)
            store_window(sz, which, proj, columns[1], jnp.where(first, grad_keys[:length], grad_keys[length:]))
            store_window(sz, which, proj, columns[2], jnp.where(first, grad_values[:length], grad_values[length:]))


def attend_backward(sz, me, h_ref, normed, grad_ref, ctx_ref, proj, gain, triple, dh_ref, scratch, pack, small):
    total, turned, blocks = scratch
    width = sz.width
    grad = grad_ref[...]
    out_rows = 3 * sz.tiles * sz.cut
    turned_blocks(sz, ctx_ref[...], me, turned, blocks)
    output_grad = dot(blocks[...], grad)
    for j in range(sz.sections):
        put_tiles(pack, j, out_rows, output_grad[j * sz.cut : (j + 1) * sz.cut, :])
    turned_blocks(sz, normed[...], me, turned, blocks)
    after = 2 * sz.tiles
    for part in range(3):
        columns = slice(part * width, (part + 1) * width)
        grad_part = proj[:, columns]
        triple_grad = dot(blocks[...], grad_part)
        for j in range(sz.sections):
            put_tiles(pack, j, part * sz.tiles * sz.cut, triple_grad[j * sz.cut : (j + 1) * sz.cut, :])
        if part != 1:
            after = put_vector(small, after, jnp.sum(grad_part.astype(f32), axis=0, keepdims=True))
    total[...] = dot_last(proj[...], triple[...])
    gain_sum, shift_sum = norm_backward(sz, h_ref, grad_ref, total, gain, dh_ref)
    put_vector(small, 0, gain_sum)
    put_vector(small, sz.tiles, shift_sum)
    return put_vector(small, after, jnp.sum(grad.astype(f32), axis=0, keepdims=True))


def put_rows(sz, value, me, turned, blocks, keep, send):
    turned_blocks(sz, value, me, turned, blocks)
    for j in range(sz.sections):
        for tile in range(sz.rows // LANES):
            (keep, send)[j % 2][j // 2, tile * sz.cut : (tile + 1) * sz.cut, :] = blocks[
                j * sz.cut : (j + 1) * sz.cut, tile * LANES : (tile + 1) * LANES
            ]


def ship(exchange, me, replica, pack, rows, keep, send):
    size = rows // exchange.shards
    for shard in range(exchange.shards):
        offset = exchange.shard_of(replica) ^ shard
        for core in range(2):
            for across in range(2):
                options = [exchange.place(c, across, offset) for c in range(2)]
                place = jnp.where(me & 1 ^ core == 0, options[0], options[1])
                target = (keep, send)[core]
                target[pl.ds(pl.multiple_of(place * size, 16), size), :] = pack[
                    2 * across + core, shard * size : (shard + 1) * size, :
                ]


def put_small(pack, start, rows, small):
    held = small.shape[0]
    for j in range(pack.shape[0]):
        pack[j, start : start + held, :] = small[...].astype(bf16)
        if start + held < rows:
            pack[j, start + held : rows, :] = jnp.zeros((rows - start - held, LANES), bf16)


class Moves:
    def __init__(self, pairs, sems):
        self.copies = [pltpu.make_async_copy(source, target, sems.at[i]) for i, (source, target) in enumerate(pairs)]

    def start(self, *which):
        for i in which:
            self.copies[i].start()

    def wait(self, *which):
        for i in which:
            self.copies[i].wait()


def row_of(ref, layer):
    return ref[layer : layer + 1, :].astype(f32)


def pick_row(block, which):
    value = block[:, 0, :].astype(f32)
    for other in range(1, block.shape[1]):
        value = jnp.where(which == other, block[:, other, :].astype(f32), value)
    return value


def gather_rows(sz, of_global, of_local, crop, image, wide):
    wide[: sz.global_len, :] = pick_row(of_global, crop)
    for at in range(sz.locals):
        start = sz.global_len + at * sz.local_len
        wide[start : start + sz.local_len, :] = pick_row(of_local.at[at], image)
    wide[sz.used :, :] = jnp.zeros((sz.rows - sz.used, sz.width), f32)


def front_kernel(sz, *refs):
    rows_in, smalls_in, ratio_ref, weights_in, refs = refs[:4], refs[4:14], refs[14], refs[15:19], refs[19:]
    (
        s0, s1, s2, s3, n0, n1, n2, qkv0, qkv1, lse0, lse1, ctx0, ctx1, act0, act1, slope0, masked_ref, grad,
        triple0, triple1, output0, output1, up0, down0, down1, gain_a, gain_e, down_b, keep, send,
    ) = refs[:30]
    (
        up1, rank_ref, token_ref, shift_a, pair, output_b, shift_e, up_b, own_global, own_local, own_global_back,
        own_local_back, n3, slope1, wide, bias0, bias1, turned, blocks, pack, small, first_grad, load_sems,
    ) = refs[30:]
    own = (own_global, own_local, own_global_back, own_local_back)
    smalls = (rank_ref, token_ref, gain_a, shift_a, pair, output_b, gain_e, shift_e, up_b, down_b)
    weights = ((triple0, output0, up0, down0), (triple1, output1, up1, down1))
    me, replica = lax.axis_index("section"), lax.axis_index("dp")
    per_image = sz.sections // sz.images
    image, crop = me // per_image, me % per_image
    several = pl.ds(crop * sz.locals, sz.locals)
    places = [image, several, image, several]
    pairs = [(source.at[place], target) for source, place, target in zip(rows_in, places, own)]
    pairs += list(zip(smalls_in, smalls))
    pairs += [(weights_in[k].at[layer], weights[layer][k]) for layer in range(2) for k in range(4)]
    loads = Moves(pairs, load_sems)
    loads.start(0, 1, *range(4, 16))
    bias0[...] = window_bias(sz, 0)
    bias1[...] = window_bias(sz, 1)
    biases = (bias0, bias1)
    patches = sz.global_len - 1
    loads.wait(0, 1, *range(4, 14))
    loads.start(2, 3, *range(16, 22))
    limit = lax.div((ratio_ref[image] + 1) * patches, jnp.int32(10))
    both = rank_ref[image]
    entry = lax.broadcasted_iota(jnp.int32, both.shape, 0)
    ranks = jnp.sum(jnp.where(entry == crop, both, 0), axis=0, keepdims=True)
    shape = (sz.rows, patches)
    row = lax.broadcasted_iota(jnp.int32, shape, 0)
    column = lax.broadcasted_iota(jnp.int32, shape, 1)
    chosen = jnp.where((row == column + 1) & (ranks < limit), 1.0, 0.0)
    chosen = jnp.max(chosen, axis=-1, keepdims=True)
    masked_ref[...] = jnp.broadcast_to(chosen, masked_ref.shape)
    gather_rows(sz, own[0], own[1], crop, image, wide)
    s0[...] = jnp.where(chosen > 0.5, token_ref[...].astype(f32), wide[...]).astype(bf16)

    def attend_weights(layer):
        triple, output, _, _ = weights[layer]
        return (
            row_of(gain_a, layer), row_of(shift_a, layer), triple, row_of(pair, layer), output, row_of(output_b, layer),
        )

    def expand_weights(layer):
        return row_of(gain_e, layer), row_of(shift_e, layer), weights[layer][2], row_of(up_b, layer)

    loads.wait(14, 15)
    attend_forward(sz, s0, attend_weights(0), s1, n0, qkv0, lse0, ctx0, biases)
    loads.wait(16, 17)
    expand_hidden(sz, s1, expand_weights(0), n1, act0, slope0)
    s2[...] = expand_output(s1, act0, down0, row_of(down_b, 0)).astype(bf16)
    loads.wait(18, 19)
    attend_forward(sz, s2, attend_weights(1), s3, n2, qkv1, lse1, ctx1, biases)
    loads.wait(20, 21)
    expand_hidden(sz, s3, expand_weights(1), n3, act1, slope1)
    loads.wait(2, 3)
    gather_rows(sz, own[2], own[3], crop, image, wide)
    first_grad[...] = wide[...].astype(bf16)
    small[...] = jnp.zeros_like(small)
    expand_backward(
        sz, me, s3, n3, first_grad, act1, slope1, row_of(gain_e, 1), up1, down1, grad, (wide, turned, blocks), pack, small
    )
    rows = sz.packed(sz.expand_full)
    put_small(pack, sz.expand_full, rows, small)
    ship(sz.exchanges["A"], me, replica, pack, rows, keep, send)


def output_kernel(sz, h_ref, act_ref, down, down_b, out_keep, out_send, turned, blocks):
    me = lax.axis_index("section")
    last = expand_output(h_ref, act_ref, down, row_of(down_b, 1)).astype(bf16)
    put_rows(sz, last, me, turned, blocks, out_keep, out_send)


def expand_kernel(sz, h, normed, grad, act, slope, up, down, gain, dh_ref, keep, send, total, turned, blocks, pack, small):
    me, replica = lax.axis_index("section"), lax.axis_index("dp")
    small[...] = jnp.zeros_like(small)
    expand_backward(
        sz, me, h, normed, grad, act, slope, row_of(gain, 0), up, down, dh_ref, (total, turned, blocks), pack, small
    )
    rows = sz.packed(sz.expand_full)
    put_small(pack, sz.expand_full, rows, small)
    ship(sz.exchanges["C"], me, replica, pack, rows, keep, send)


def attend_core_kernel(sz, grad, output, qkv, lse, proj, dctx, bias0, bias1):
    bias0[...] = window_bias(sz, 0)
    bias1[...] = window_bias(sz, 1)
    attend_core_backward(sz, grad, output, qkv, lse, proj, dctx, (bias0, bias1))


def attend_kernel(sz, layer, *refs):
    h, normed, grad, ctx, proj, triple, gain, flags = refs[:8]
    if layer == 0:
        in_keep, in_send, keep, send, total, turned, blocks, pack, small = refs[8:]
        target = total
    else:
        target, keep, send, total, turned, blocks, pack, small = refs[8:]
    me, replica = lax.axis_index("section"), lax.axis_index("dp")
    small[...] = jnp.zeros_like(small)
    rows = sz.packed(sz.attend_full)
    after = attend_backward(
        sz, me, h, normed, grad, ctx, proj, row_of(gain, layer), triple, target, (total, turned, blocks), pack, small
    )
    if layer == 0:
        masked = flags[:, :1] > 0.5
        put_vector(small, after, jnp.sum(jnp.where(masked, total[...], 0.0), axis=0, keepdims=True))
        put_rows(sz, jnp.where(masked, 0.0, total[...]).astype(bf16), me, turned, blocks, in_keep, in_send)
    put_small(pack, sz.attend_full, rows, small)
    ship(sz.exchanges["DB"[layer]], me, replica, pack, rows, keep, send)


def unpack(exchange, me, replica, source, target):
    shard = target.shape[0] // exchange.shards
    for place in range(exchange.shards):
        options = [exchange.offset(core, place) for core in range(2)]
        offset = jnp.where(me & 1 == 0, options[0], options[1])
        at = pl.multiple_of((exchange.shard_of(replica) ^ offset) * shard, 16)
        target[pl.ds(at, shard), :] = source[place * shard : (place + 1) * shard, :]


def widen_tiles(source, base, target):
    r, columns = target.shape
    for tile in range(columns // LANES):
        target[:, tile * LANES : (tile + 1) * LANES] = source[base + tile * r : base + (tile + 1) * r, :].astype(f32)


def widen(sz, attend, expand, targets, moves):
    triple, output, up, down = targets
    hidden_rows = sz.hidden // LANES * sz.cut
    for index, (source, base, target) in enumerate(
        ((expand, 0, up), (expand, hidden_rows, down), (attend, 0, triple), (attend, 3 * sz.tiles * sz.cut, output))
    ):
        widen_tiles(source, base, target)
        moves[(2, 3, 0, 1)[index]].start()


def early_kernel(sz, *refs):
    (expand_in, attend_in), (out_own, out_core, in_own, in_core, across) = refs[:2], refs[2:7]
    (out_global, out_local, in_global, in_local), outs, vectors = refs[7:11], refs[11:15], refs[15]
    expand, attend, targets, wide, sems = refs[16], refs[17], refs[18:22], refs[22], refs[23]
    me, replica = lax.axis_index("section"), lax.axis_index("dp")
    moves = [pltpu.make_async_copy(target, out.at[1], sems.at[i]) for i, (target, out) in enumerate(zip(targets, outs))]
    unpack(sz.exchanges["A"], me, replica, expand_in, expand)
    unpack(sz.exchanges["B"], me, replica, attend_in, attend)
    widen(sz, attend, expand, targets, moves)
    vectors[: sz.small_rows, :] = attend[sz.attend_full : sz.attend_full + sz.small_rows, :].astype(f32)
    vectors[sz.small_rows :, :] = expand[sz.expand_full : sz.expand_full + sz.small_rows, :].astype(f32)
    row_parts = (
        (out_own.at[0], out_core.at[0], across.at[0], across.at[1]),
        (in_own.at[0], in_core.at[0], across.at[2], across.at[3]),
    )
    per_image = sz.sections // sz.images
    for which, (to_global, to_local) in enumerate(((out_global, out_local), (in_global, in_local))):
        for k in range(4):
            section = me ^ k
            image, crop = section // per_image, section % per_image
            turned = jnp.concatenate(
                [
                    row_parts[which][k][tile * sz.cut : (tile + 1) * sz.cut, :].astype(f32)
                    for tile in range(sz.rows // LANES)
                ],
                axis=1,
            )
            to_global[section] = turned[:, : sz.global_len]
            turned = jnp.concatenate([turned, jnp.zeros((LANES - sz.cut, sz.rows), f32)], axis=0)
            wide[...] = turned.T
            for at in range(sz.locals):
                start = sz.global_len + at * sz.local_len
                to_local[crop * sz.locals + at, :, pl.ds(image, 1), :] = wide[
                    start : start + sz.local_len, : sz.cut
                ].reshape(sz.local_len, 1, sz.cut)
    for move in moves:
        move.wait()


def finish_kernel(sz, *refs):
    expand_in, attend_in, later_vectors = refs[:3]
    (token, gain_a, shift_a, pair, output_b, gain_e, shift_e, up_b, down_b), outs = refs[7:16], refs[16:20]
    expand, attend, targets, vectors, sems = refs[20], refs[21], refs[22:26], refs[26], refs[27]
    me, replica = lax.axis_index("section"), lax.axis_index("dp")
    moves = [pltpu.make_async_copy(target, out.at[0], sems.at[i]) for i, (target, out) in enumerate(zip(targets, outs))]
    unpack(sz.exchanges["C"], me, replica, expand_in, expand)
    unpack(sz.exchanges["D"], me, replica, attend_in, attend)
    widen(sz, attend, expand, targets, moves)
    width, tiles, cut = sz.width, sz.tiles, sz.cut
    row = lax.broadcasted_iota(jnp.int32, (width, cut), 0)
    column = lax.broadcasted_iota(jnp.int32, (width, cut), 1)
    pick = jnp.where(row == column + me * cut, 1.0, 0.0).astype(bf16)
    row = lax.broadcasted_iota(jnp.int32, (2 * width, 2 * cut), 0)
    column = lax.broadcasted_iota(jnp.int32, (2 * width, 2 * cut), 1)
    pick_pair = jnp.where(row == column + me * 2 * cut, 1.0, 0.0).astype(bf16)
    hidden_tiles, up_tiles = sz.hidden // LANES, sz.hidden_cut // LANES
    vectors[: sz.small_rows, :] = attend[sz.attend_full : sz.attend_full + sz.small_rows, :].astype(f32)
    vectors[sz.small_rows :, :] = expand[sz.expand_full : sz.expand_full + sz.small_rows, :].astype(f32)
    for layer, held in enumerate((vectors, later_vectors)):
        one = slice(layer, layer + 1)

        def vector(at, tiles_in):
            return jnp.concatenate([held[at + t : at + t + 1, :] for t in range(tiles_in)], axis=1)

        def picked(at):
            return dot(vector(at, tiles).astype(bf16), pick)

        gain_a[one, :] = picked(0)
        shift_a[one, :] = picked(tiles)
        pair[one, :] = dot(vector(2 * tiles, 2 * tiles).astype(bf16), pick_pair)
        output_b[one, :] = picked(4 * tiles)
        if layer == 0:
            token[...] = picked(5 * tiles)
        base = sz.small_rows
        gain_e[one, :] = picked(base)
        shift_e[one, :] = picked(base + tiles)
        for tile in range(up_tiles):
            up_b[one, tile * LANES : (tile + 1) * LANES] = held[pl.ds(base + 2 * tiles + me * up_tiles + tile, 1), :]
        down_b[one, :] = picked(base + 2 * tiles + hidden_tiles)
    for move in moves:
        move.wait()


VMEM = pl.BlockSpec(memory_space=pltpu.VMEM)
ANY = pl.BlockSpec(memory_space=pl.ANY)
HBM = pl.BlockSpec(memory_space=pltpu.HBM)
SMEM = pl.BlockSpec(memory_space=pltpu.SMEM)
DMA = pltpu.SemaphoreType.DMA


def call(body, name, outs, in_specs, scratch, args, flops, aliases=()):
    args = [
        pltpu.with_memory_space_constraint(arg, pltpu.HBM) if spec is HBM else arg for arg, spec in zip(args, in_specs)
    ]
    return pl.pallas_call(
        body,
        name=name,
        out_shape=tuple(jax.ShapeDtypeStruct(shape, kind) for shape, kind, _ in outs),
        in_specs=in_specs,
        out_specs=tuple(memory for _, _, memory in outs),
        scratch_shapes=[pltpu.VMEM(*item) if isinstance(item, tuple) else item for item in scratch],
        input_output_aliases=dict(aliases),
        compiler_params=pltpu.CompilerParams(vmem_limit_bytes=VMEM_MIB.get(name, 14) << 20),
        cost_estimate=pl.CostEstimate(flops=flops, bytes_accessed=1 << 20, transcendentals=0),
    )(*args)


def add(first, *others):
    total = first.astype(f32)
    for other in others:
        total = total + other.astype(f32)
    return lax.reduce_precision(total, 8, 7).astype(bf16)


def swap(value, partner_of):
    sections, replicas = lax.axis_size("section"), lax.axis_size("dp")
    route = []
    for section in range(sections):
        for replica in range(replicas):
            to_section, to_replica = partner_of(section, replica)
            route.append((section * replicas + replica, to_section * replicas + to_replica))
    return lax.ppermute(value, ("section", "dp"), route)


def other_core(section, replica):
    return section ^ 1, replica


def other_x(section, replica):
    return section ^ 2, replica


def along(orders, step):
    def partner_of(section, replica):
        axis = orders[section & 1][step]
        return (section ^ 2, replica) if axis == X_AXIS else (section, replica ^ (1 << axis))

    return partner_of


class Sequence:
    def __init__(self):
        self.last = None

    def after(self, value):
        return value if self.last is None else lax.optimization_barrier((value, self.last))[0]

    def mark(self, value):
        self.last = value
        return value


def reduce_steps(exchange, order, keep, send):
    orders = exchange.orders
    core = swap(send, other_core)
    yield
    core = order.after(core)
    half = keep.shape[0] // 2
    moved = swap(order.mark(add(keep[half:], core[half:])), along(orders, 0))
    yield
    moved = order.after(moved)
    mine = add(keep[:half], core[:half], moved)
    for step in range(1, len(orders[0])):
        half = mine.shape[0] // 2
        moved = swap(order.mark(mine[half:]), along(orders, step))
        yield
        mine = add(mine[:half], order.after(moved))
    for axis in exchange.rest:
        moved = swap(order.mark(mine), along(([axis], [axis]), 0))
        yield
        mine = add(mine, order.after(moved))
    back = [[axis for axis in order_of if axis != X_AXIS] for order_of in orders]
    for step in reversed(range(len(back[0]))):
        moved = swap(order.mark(mine), along(back, step))
        yield
        mine = jnp.concatenate([mine, order.after(moved)], axis=0)
    yield mine


def row_steps(order, out_rows, in_rows):
    cores = [swap(send, other_core) for _, send in (out_rows, in_rows)]
    yield
    cores[0] = order.after(cores[0])
    across = swap(order.mark(jnp.stack([out_rows[0][1], cores[0][1], in_rows[0][1], cores[1][1]])), other_x)
    yield
    yield out_rows[0], cores[0], in_rows[0], cores[1], order.after(across)


def per_device(
    global_rows, local_rows, patch_rank, ratio_bin, mask_token, attend_gain, attend_shift, triple_weight,
    pair_bias, output_weight, output_bias, expand_gain, expand_shift, up_weight, up_bias, down_weight,
    down_bias, grad_global, grad_local,
):
    sections, replicas = lax.axis_size("section"), lax.axis_size("dp")
    sz = Sizes(global_rows, local_rows, up_weight, sections, replicas)
    width, rows, hidden = sz.width, sz.rows, sz.hidden
    sets = [rows_of.transpose(0, 2, 1, 3) for rows_of in (global_rows, grad_global)]
    many = [rows_of.transpose(1, 2, 0, 3) for rows_of in (local_rows, grad_local)]
    weights = (triple_weight, output_weight, up_weight, down_weight)
    smalls = (
        patch_rank, mask_token, attend_gain, attend_shift, pair_bias, output_bias, expand_gain, expand_shift, up_bias,
        down_bias,
    )
    wide = ((rows, width), bf16)
    triple_rows = ((rows, 3 * width), bf16)
    hidden_rows = ((rows, hidden), bf16)
    lse = ((16, up_to(max(length for _, length in sz.windows), LANES)), f32)
    flags = ((rows, LANES), f32)
    wide_f32 = ((rows, width), f32)
    turned = ((width, rows), bf16)
    small = ((sz.small_rows, LANES), f32)
    share = ((2, sz.extra, LANES), bf16)
    stage = ((sections, sz.extra, LANES), bf16)
    windows = [((length, length), f32) for _, length in sz.windows]
    totals = [sz.packed(full) for full in (sz.expand_full, sz.attend_full)]
    packs = [((sections, total, LANES), bf16) for total in totals]
    parts = [((2 * total, LANES), bf16) for total in totals]
    vectors = ((2, width), bf16)
    blocks = [(weight.shape[1:], bf16) for weight in weights]
    shared = [wide_f32, turned, turned]

    def run_kernel(body, name, outs, scratch, args):
        return call(
            lambda *refs: body(sz, *refs), name, [out + (VMEM,) for out in outs], [VMEM] * len(args), scratch, args, 4 << 30
        )

    (
        s0, s1, s2, s3, n0, n1, n2, qkv0, qkv1, lse0, lse1, ctx0, ctx1, act0, act1, slope0, masked, grad,
        triple0, triple1, output0, output1, up0, down0, down1, gain_a, gain_e, down_b, keep, send,
    ) = call(
        lambda *refs: front_kernel(sz, *refs),
        "front",
        [
            out + (VMEM,)
            for out in [wide] * 7 + [triple_rows] * 2 + [lse] * 2 + [wide] * 2 + [hidden_rows] * 3 + [flags, wide]
            + [blocks[0]] * 2 + [blocks[1]] * 2 + [blocks[2]] + [blocks[3]] * 2 + [vectors] * 3 + [parts[0]] * 2
        ],
        [HBM] * 14 + [SMEM] + [HBM] * 4,
        [blocks[2]]
        + [(one.shape, one.dtype) for one in (patch_rank, mask_token, attend_shift, pair_bias, output_bias)]
        + [(one.shape, one.dtype) for one in (expand_shift, up_bias)]
        + [(sets[0].shape[1:], bf16), ((sz.locals,) + many[0].shape[1:], bf16)] * 2
        + [wide, hidden_rows, wide_f32] + windows + [turned] * 2 + [packs[0], small, wide, DMA((22,))],
        (sets[0], many[0], sets[1], many[1], *smalls, ratio_bin, *weights),
        8 << 30,
    )
    order = Sequence()
    chains, results = {}, {}
    chains["A"] = reduce_steps(sz.exchanges["A"], order, keep, send)
    core_scratch = [wide] + windows
    flow = {"grad": grad}

    def core_kernel(name, output, qkv, lse_of):
        proj, = run_kernel(
            attend_core_kernel, name, [triple_rows], core_scratch, (order.after(flow["grad"]), output, qkv, lse_of)
        )
        flow["proj"] = order.mark(proj)

    def later_core():
        core_kernel("later_core", output1, qkv1, lse1)

    def later_attend():
        dh, keep, send = run_kernel(
            lambda sz, *refs: attend_kernel(sz, 1, *refs), "later_attend", [wide] + [parts[1]] * 2,
            shared + [packs[1], small],
            (s2, n2, flow["grad"], ctx1, order.after(flow["proj"]), triple1, gain_a, masked),
        )
        flow["grad"] = order.mark(dh)
        chains["B"] = reduce_steps(sz.exchanges["B"], order, keep, send)

    def expand():
        dh, keep, send = run_kernel(
            expand_kernel, "expand_back", [wide] + [parts[0]] * 2, shared + [packs[0], small],
            (s1, n1, order.after(flow["grad"]), act0, slope0, up0, down0, gain_e),
        )
        flow["grad"] = order.mark(dh)
        chains["C"] = reduce_steps(sz.exchanges["C"], order, keep, send)

    def core():
        core_kernel("attend_core", output0, qkv0, lse0)

    def attend():
        in_keep, in_send, keep, send = run_kernel(
            lambda sz, *refs: attend_kernel(sz, 0, *refs), "attend_back", [share] * 2 + [parts[1]] * 2,
            shared + [packs[1], small],
            (s0, n0, flow["grad"], ctx0, order.after(flow["proj"]), triple0, gain_a, masked),
        )
        flow["in"] = (order.mark(in_keep), in_send)
        chains["D"] = reduce_steps(sz.exchanges["D"], order, keep, send)

    def output_rows():
        out_rows = run_kernel(
            output_kernel, "output_rows", [share] * 2, [turned, turned], (s3, order.after(act1), down1, down_b)
        )
        order.mark(out_rows[0])
        chains["R"] = row_steps(order, out_rows, flow["in"])

    cut = sz.cut
    weight_outs = [(2, cut, 3 * width), (2, cut, width), (2, cut, hidden), (2, sz.hidden_cut, width)]
    row_outs = [(sz.all_globals, cut, sz.global_len), local_rows.shape[1:3] + (sz.images, cut)] * 2
    both_small = ((2 * sz.small_rows, LANES), f32)
    finish_scratch = [((total, LANES), bf16) for total in totals] + [(shape[1:], f32) for shape in weight_outs]

    def early():
        expand_of, attend_of = (order.after(results[step]) for step in "AB")
        flow["early"] = call(
            lambda *refs: early_kernel(sz, *refs), "early",
            [(shape, f32, VMEM) for shape in row_outs] + [(shape, f32, ANY) for shape in weight_outs] + [both_small + (VMEM,)],
            [VMEM] * 7, finish_scratch + [flags, DMA((4,))], (expand_of, attend_of, *results["R"]), 1 << 28,
        )
        order.mark(flow["early"][-1])

    kernels = {
        "later_core": later_core, "later_attend": later_attend, "expand": expand, "core": core, "attend": attend,
        "output": output_rows, "early": early,
    }
    for plan in PLAN:
        for step in plan.split():
            if step == "early":
                for _ in range(3, len(sz.exchanges["A"].rest) + len(sz.exchanges["A"].axes)):
                    for name in "ABCD":
                        results[name] = next(chains[name], results.get(name))
            if step in kernels:
                kernels[step]()
            else:
                results[step] = next(chains[step], results.get(step))
    *row_values, triple, output, up, down, late_vectors = flow["early"]
    vector_outs = [(1, cut), (2, cut), (2, cut), (2, 2 * cut)] + [(2, cut)] * 3 + [(2, sz.hidden_cut), (2, cut)]
    final = call(
        lambda *refs: finish_kernel(sz, *refs), "finish",
        [(shape, f32, VMEM) for shape in vector_outs] + [(shape, f32, ANY) for shape in weight_outs],
        [VMEM] * 3 + [ANY] * 4, finish_scratch + [both_small, DMA((4,))],
        (order.after(results["C"]), results["D"], late_vectors, triple, output, up, down), 1 << 28,
        [(3 + i, len(vector_outs) + i) for i in range(4)],
    )
    token, gain_a, shift_a, pair, output_b, gain_e, shift_e, up_b, down_b, triple, output, up, down = final
    shape = global_rows.shape[:2] + (cut, sz.global_len)
    return (
        row_values[0].reshape(shape).transpose(0, 1, 3, 2), row_values[1].transpose(2, 0, 1, 3),
        row_values[2].reshape(shape).transpose(0, 1, 3, 2), row_values[3].transpose(2, 0, 1, 3),
        token, gain_a, shift_a, triple, pair, output, output_b, gain_e, shift_e, up, up_b, down, down_b,
    )


def solution(mesh):
    rows, copied = P("dp", None, None, None), P()
    in_specs = (rows, rows, P("dp", None, None), P("dp")) + (copied,) * 13 + (rows, rows)
    wide, flat, deep = P("dp", None, None, "section"), P(None, "section"), P(None, "section", None)
    out_specs = (
        wide, wide, wide, wide, flat, flat, flat, deep, flat, deep, flat, flat, flat, deep, flat, deep, flat,
    )
    return jax.shard_map(per_device, mesh=mesh, in_specs=in_specs, out_specs=out_specs, check_vma=False)
```

profile of v0, /device:TPU:0, one launch (start us, length us, event | category | flops | bytes accessed | tf_op | source)
XLA Modules:
  0.0 96.1 jit_solution(11823118583616467002)
XLA Ops:
  1.3 16.0 %front.1 = (bf16[384,384]{1,0:T(8,128)(2,1)S(1)}, bf16[384,384]{1,0:T(8,128)(2,1)S(1)}, bf16[384,384]{1,0:T(8,128)(2,1)S(1)}, bf16[384,384]{1,0:T(8,128)(2,1)S(1...) custom-call(bf16[2,197,2,384]{3,2,1,0:T(2,128)(2,1)} %bitcast.12, ...), custom_call_target="tpu_custom_call" | custom-call | flops 8589934592 | bytes 1048576 | tf_op jit(solution)/shard_map/front/pallas_call | solution.py:656
  17.8 2.8 %later_core.1.refs_4_ = bf16[384,1152]{1,0:T(8,128)(2,1)S(1)} custom-call(bf16[384,384]{1,0:T(8,128)(2,1)S(1)} %get-tuple-element.122.refs_0_.refs_2_, bf16[384,384]{1,0:T(8,128)(2,1)S(1)} %get-tuple-element.124.refs_1_, bf16[384,1152]{1,0:T(8,128)(2,1)S(1)} %get-tuple-element.125.refs_2_, f32[16,256]{1,0:T(8,128)S(1)} %get-tuple-element.126.refs_3_), custom_call_target="tpu_custom_call" | custom-call | flops 4294967296 | bytes 1048576 | tf_op jit(solution)/shard_map/later_core/pallas_call | solution.py:656
  20.6 2.0 %later_attend.1 = (bf16[384,384]{1,0:T(8,128)(2,1)S(1)}, bf16[2432,128]{1,0:T(8,128)(2,1)S(1)}, bf16[2432,128]{1,0:T(8,128)(2,1)S(1)}) custom-call(bf16[384,384]{1,0:T(8,128)(2,1)S(1)} %get-tuple-element.120.refs_0_, bf16[384,384]{1,0:T(8,128)(2,1)S(1)} %get-tuple-element.121.refs_1_, bf16[384,384]{1,0:T(8,128)(2,1)S(1)} %get-tuple-element.122.refs_0_.refs_2_, ...), custom_call_target="tpu_custom_call" | custom-call | flops 4294967296 | bytes 1048576 | tf_op jit(solution)/shard_map/later_attend/pallas_call | solution.py:656
  22.8 2.6 %collective-permute-start.1 = (bf16[2368,128]{1,0:T(8,128)(2,1)S(1)}, bf16[2368,128]{1,0:T(8,128)(2,1)S(1)}, u32[]{:S(2)}, u32[]{:S(2)}) collective-permute-start(bf16[2368,128]{1,0:T(8,128)(2,1)S(1)} %reduce-precision_convert_fusion.3), channel_id=1, source_target_pairs={{0,16},{1,17},{2,18},{3,19},{4,20},{5,21},{6,22},{7,23},{8,10},{9,... | collective-permute-start | bytes 1818632 | tf_op jit(solution)/shard_map/ppermute | solution.py:683
  25.4 4.0 %expand_back.1 = (bf16[384,384]{1,0:T(8,128)(2,1)S(1)}, bf16[4736,128]{1,0:T(8,128)(2,1)S(1)}, bf16[4736,128]{1,0:T(8,128)(2,1)S(1)}) custom-call(bf16[384,384]{1,0:T(8,128)(2,1)S(1)} %get-tuple-element.132.refs_0_, bf16[384,384]{1,0:T(8,128)(2,1)S(1)} %get-tuple-element.133.refs_1_, bf16[384,384]{1,0:T(8,128)(2,1)S(1)} %get-tuple-element.134.refs_2_, ...), custom_call_target="tpu_custom_call" | custom-call | flops 4294967296 | bytes 1048576 | tf_op jit(solution)/shard_map/expand_back/pallas_call | solution.py:656
  29.9 2.8 %attend_core.1.refs_4_ = bf16[384,1152]{1,0:T(8,128)(2,1)S(1)} custom-call(bf16[384,384]{1,0:T(8,128)(2,1)S(1)} %get-tuple-element.141.refs_0_.refs_2_, bf16[384,384]{1,0:T(8,128)(2,1)S(1)} %get-tuple-element.142.refs_1_, bf16[384,1152]{1,0:T(8,128)(2,1)S(1)} %get-tuple-element.143.refs_2_, f32[16,256]{1,0:T(8,128)S(1)} %get-tuple-element.144.refs_3_), custom_call_target="tpu_custom_call" | custom-call | flops 4294967296 | bytes 1048576 | tf_op jit(solution)/shard_map/attend_core/pallas_call | solution.py:656
  34.1 2.1 %collective-permute-start.6 = (bf16[2368,128]{1,0:T(8,128)(2,1)S(1)}, bf16[2368,128]{1,0:T(8,128)(2,1)S(1)}, u32[]{:S(2)}, u32[]{:S(2)}) collective-permute-start(bf16[2368,128]{1,0:T(8,128)(2,1)S(1)} %reduce-precision_convert_fusion.1), channel_id=1, source_target_pairs={{0,1},{1,0},{2,3},{3,2},{4,5},{5,4},{6,7},{7,6},{8,10},{9,11},{10,... | collective-permute-start | bytes 1818632 | tf_op jit(solution)/shard_map/ppermute | solution.py:683
  36.3 2.2 %attend_back.1 = (bf16[2,288,128]{2,1,0:T(8,128)(2,1)S(1)}, bf16[2,288,128]{2,1,0:T(8,128)(2,1)S(1)}, bf16[2432,128]{1,0:T(8,128)(2,1)S(1)}, bf16[2432,128]{1,0:T(8,128)(2,1)S(1)}) custom-call(bf16[384,384]{1,0:T(8,128)(2,1)S(1)} %get-tuple-element.146.refs_0_, bf16[384,384]{1,0:T(8,128)(2,1)S(1)} %get-tuple-element.147.refs_1_, ...), custom_call_target="tpu_custom_call" | custom-call | flops 4294967296 | bytes 1048576 | tf_op jit(solution)/shard_map/attend_back/pallas_call | solution.py:656
  41.6 2.6 %collective-permute-done.6 = bf16[2368,128]{1,0:T(8,128)(2,1)S(1)} collective-permute-done((bf16[2368,128]{1,0:T(8,128)(2,1)S(1)}, bf16[2368,128]{1,0:T(8,128)(2,1)S(1)}, u32[]{:S(2)}, u32[]{:S(2)}) %collective-permute-start.6) | collective-permute-done | bytes 606240 | tf_op jit(solution)/shard_map/ppermute | solution.py:683
  44.5 2.1 %collective-permute-start.12 = (bf16[1184,128]{1,0:T(8,128)(2,1)S(1)}, bf16[1184,128]{1,0:T(8,128)(2,1)S(1)}, u32[]{:S(2)}, u32[]{:S(2)}) collective-permute-start(bf16[1184,128]{1,0:T(8,128)(2,1)S(1)} %slice.146), channel_id=1, source_target_pairs={{0,16},{1,17},{2,18},{3,19},{4,20},{5,21},{6,22},{7,23},{8,24},{9,... | collective-permute-start | bytes 909320 | tf_op jit(solution)/shard_map/ppermute | solution.py:683
  47.6 2.1 %collective-permute-start.7 = (bf16[592,128]{1,0:T(8,128)(2,1)S(1)}, bf16[592,128]{1,0:T(8,128)(2,1)S(1)}, u32[]{:S(2)}, u32[]{:S(2)}) collective-permute-start(bf16[592,128]{1,0:T(8,128)(2,1)S(1)} %slice.148), channel_id=1, source_target_pairs={{0,2},{1,3},{2,0},{3,1},{4,6},{5,7},{6,4},{7,5},{8,9},{9,8},{10,11... | collective-permute-start | bytes 454664 | tf_op jit(solution)/shard_map/ppermute | solution.py:683
  52.9 3.1 %collective-permute-start.9 = (bf16[592,128]{1,0:T(8,128)(2,1)S(1)}, bf16[592,128]{1,0:T(8,128)(2,1)S(1)}, u32[]{:S(2)}, u32[]{:S(2)}) collective-permute-start(bf16[592,128]{1,0:T(8,128)(2,1)S(1)} %reduce-precision_convert_fusion.15), channel_id=1, source_target_pairs={{0,4},{1,5},{2,6},{3,7},{4,0},{5,1},{6,2},{7,3},{8,12},{9,13},{10,... | collective-permute-start | bytes 454664 | tf_op jit(solution)/shard_map/ppermute | solution.py:683
  56.1 1.7 %collective-permute-start.11 = (bf16[304,128]{1,0:T(8,128)(2,1)S(1)}, bf16[304,128]{1,0:T(8,128)(2,1)S(1)}, u32[]{:S(2)}, u32[]{:S(2)}) collective-permute-start(bf16[304,128]{1,0:T(8,128)(2,1)S(1)} %slice.152), channel_id=1, source_target_pairs={{0,2},{1,3},{2,0},{3,1},{4,6},{5,7},{6,4},{7,5},{8,9},{9,8},{10,11... | collective-permute-start | bytes 233480 | tf_op jit(solution)/shard_map/ppermute | solution.py:683
  57.7 2.0 %collective-permute-done.13 = bf16[1216,128]{1,0:T(8,128)(2,1)S(1)} collective-permute-done((bf16[1216,128]{1,0:T(8,128)(2,1)S(1)}, bf16[1216,128]{1,0:T(8,128)(2,1)S(1)}, u32[]{:S(2)}, u32[]{:S(2)}) %collective-permute-start.13) | collective-permute-done | bytes 311328 | tf_op jit(solution)/shard_map/ppermute | solution.py:683
  60.5 1.7 %collective-permute-start.17 = (bf16[592,128]{1,0:T(8,128)(2,1)S(1)}, bf16[592,128]{1,0:T(8,128)(2,1)S(1)}, u32[]{:S(2)}, u32[]{:S(2)}) collective-permute-start(bf16[592,128]{1,0:T(8,128)(2,1)S(1)} %slice.155), channel_id=1, source_target_pairs={{0,2},{1,3},{2,0},{3,1},{4,6},{5,7},{6,4},{7,5},{8,9},{9,8},{10,11... | collective-permute-start | bytes 454664 | tf_op jit(solution)/shard_map/ppermute | solution.py:683
  62.2 2.7 %collective-permute-start.15 = (bf16[304,128]{1,0:T(8,128)(2,1)S(1)}, bf16[304,128]{1,0:T(8,128)(2,1)S(1)}, u32[]{:S(2)}, u32[]{:S(2)}) collective-permute-start(bf16[304,128]{1,0:T(8,128)(2,1)S(1)} %reduce-precision_convert_fusion.19), channel_id=1, source_target_pairs={{0,4},{1,5},{2,6},{3,7},{4,0},{5,1},{6,2},{7,3},{8,12},{9,13},{10,... | collective-permute-start | bytes 233480 | tf_op jit(solution)/shard_map/ppermute | solution.py:683
  66.5 2.6 %collective-permute-start.23 = (bf16[592,128]{1,0:T(8,128)(2,1)S(1)}, bf16[592,128]{1,0:T(8,128)(2,1)S(1)}, u32[]{:S(2)}, u32[]{:S(2)}) collective-permute-start(bf16[592,128]{1,0:T(8,128)(2,1)S(1)} %reduce-precision_convert_fusion.13), channel_id=1, source_target_pairs={{0,4},{1,5},{2,6},{3,7},{4,0},{5,1},{6,2},{7,3},{8,12},{9,13},{10,... | collective-permute-start | bytes 454664 | tf_op jit(solution)/shard_map/ppermute | solution.py:683
  69.2 2.5 %collective-permute-start.19 = (bf16[304,128]{1,0:T(8,128)(2,1)S(1)}, bf16[304,128]{1,0:T(8,128)(2,1)S(1)}, u32[]{:S(2)}, u32[]{:S(2)}) collective-permute-start(bf16[304,128]{1,0:T(8,128)(2,1)S(1)} %slice.158), channel_id=1, source_target_pairs={{0,2},{1,3},{2,0},{3,1},{4,6},{5,7},{6,4},{7,5},{8,9},{9,8},{10,11... | collective-permute-start | bytes 233480 | tf_op jit(solution)/shard_map/ppermute | solution.py:683
  71.9 2.3 %collective-permute-start.18 = (bf16[1184,128]{1,0:T(8,128)(2,1)S(1)}, bf16[1184,128]{1,0:T(8,128)(2,1)S(1)}, u32[]{:S(2)}, u32[]{:S(2)}) collective-permute-start(bf16[1184,128]{1,0:T(8,128)(2,1)S(1)} %pad_maximum_fusion.4), channel_id=1, source_target_pairs={{0,1},{1,0},{2,3},{3,2},{4,5},{5,4},{6,7},{7,6},{8,10},{9,11},{10,... | collective-permute-start | bytes 909320 | tf_op jit(solution)/shard_map/ppermute | solution.py:683
  74.2 2.1 %collective-permute-done.19 = bf16[304,128]{1,0:T(8,128)(2,1)S(1)} collective-permute-done((bf16[304,128]{1,0:T(8,128)(2,1)S(1)}, bf16[304,128]{1,0:T(8,128)(2,1)S(1)}, u32[]{:S(2)}, u32[]{:S(2)}) %collective-permute-start.19) | collective-permute-done | bytes 77856 | tf_op jit(solution)/shard_map/ppermute | solution.py:683
  76.3 1.9 %collective-permute-start.20 = (bf16[304,128]{1,0:T(8,128)(2,1)S(1)}, bf16[304,128]{1,0:T(8,128)(2,1)S(1)}, u32[]{:S(2)}, u32[]{:S(2)}) collective-permute-start(bf16[304,128]{1,0:T(8,128)(2,1)S(1)} %reduce-precision_convert_fusion.17), channel_id=1, source_target_pairs={{0,4},{1,5},{2,6},{3,7},{4,0},{5,1},{6,2},{7,3},{8,12},{9,13},{10,... | collective-permute-start | bytes 233480 | tf_op jit(solution)/shard_map/ppermute | solution.py:683
  79.8 1.6 %collective-permute-start.28 = (bf16[4,288,128]{2,1,0:T(8,128)(2,1)S(1)}, bf16[4,288,128]{2,1,0:T(8,128)(2,1)S(1)}, u32[]{:S(2)}, u32[]{:S(2)}) collective-permute-start(bf16[4,288,128]{2,1,0:T(8,128)(2,1)S(1)} %pad_maximum_fusion.6), channel_id=1, source_target_pairs={{0,16},{1,17},{2,18},{3,19},{4,20},{5,21},{6,22},{7,23},{8,24},{9,... | collective-permute-start | bytes 884744 | tf_op jit(solution)/shard_map/ppermute | solution.py:683
  89.1 3.2 %early.1 = (f32[4,96,197]{2,1,0:T(8,128)}, f32[10,37,2,96]{3,2,1,0:T(2,128)}, f32[4,96,197]{2,1,0:T(8,128)}, f32[10,37,2,96]{3,2,1,0:T(2,128)}, f32[2,96,1152]{2...) custom-call(bf16[2368,128]{1,0:T(8,128)(2,1)S(1)} %pad_maximum_fusio, ...), custom_call_target="tpu_custom_call" | custom-call | flops 268435456 | bytes 1048576 | tf_op jit(solution)/shard_map/early/pallas_call | solution.py:656
  93.7 2.3 %finish.1 = (f32[1,96]{1,0:T(1,128)}, f32[2,96]{1,0:T(2,128)}, f32[2,96]{1,0:T(2,128)}, f32[2,192]{1,0:T(2,128)}, f32[2,96]{1,0:T(2,128)}, /*index=5*/f32[2,96]{...) custom-call(bf16[2368,128]{1,0:T(8,128)(2,1)S(1)} %pad_maximum_fusio, ...), custom_call_target="tpu_custom_call", output_to_operand_aliasing={{9}: (3, {}), {10}: (4, {}), {11}: (5, {}), {12}: (6, {})} | custom-call | flops 268435456 | bytes 1048576 | tf_op jit(solution)/shard_map/finish/pallas_call | solution.py:656
  (95 shorter events, 24.0 us)
Async XLA Ops:
  22.8 10.6 %collective-permute-start.1 = (bf16[2368,128]{1,0:T(8,128)(2,1)S(1)}, bf16[2368,128]{1,0:T(8,128)(2,1)S(1)}, u32[]{:S(2)}, u32[]{:S(2)}) collective-permute-start(bf16[2368,128]{1,0:T(8,128)(2,1)S(1)} %reduce-precision_convert_fusion.3), channel_id=1, source_target_pairs={{0,16},{1,17},{2,18},{3,19},{4,20},{5,21},{6,22},{7,23},{8,10},{9,... | collective-permute-start | bytes 1818632 | tf_op jit(solution)/shard_map/ppermute | solution.py:683
  29.7 6.5 %collective-permute-start.3 = (bf16[2432,128]{1,0:T(8,128)(2,1)S(1)}, bf16[2432,128]{1,0:T(8,128)(2,1)S(1)}, u32[]{:S(2)}, u32[]{:S(2)}) collective-permute-start(bf16[2432,128]{1,0:T(8,128)(2,1)S(1)} %get-tuple-element.150), channel_id=1, source_target_pairs={{0,8},{1,9},{2,10},{3,11},{4,12},{5,13},{6,14},{7,15},{8,0},{9,1},... | collective-permute-start | bytes 1867784 | tf_op jit(solution)/shard_map/ppermute | solution.py:683
  34.1 10.1 %collective-permute-start.6 = (bf16[2368,128]{1,0:T(8,128)(2,1)S(1)}, bf16[2368,128]{1,0:T(8,128)(2,1)S(1)}, u32[]{:S(2)}, u32[]{:S(2)}) collective-permute-start(bf16[2368,128]{1,0:T(8,128)(2,1)S(1)} %reduce-precision_convert_fusion.1), channel_id=1, source_target_pairs={{0,1},{1,0},{2,3},{3,2},{4,5},{5,4},{6,7},{7,6},{8,10},{9,11},{10,... | collective-permute-start | bytes 1818632 | tf_op jit(solution)/shard_map/ppermute | solution.py:683
  38.6 8.9 %collective-permute-start.2 = (bf16[1184,128]{1,0:T(8,128)(2,1)S(1)}, bf16[1184,128]{1,0:T(8,128)(2,1)S(1)}, u32[]{:S(2)}, u32[]{:S(2)}) collective-permute-start(bf16[1184,128]{1,0:T(8,128)(2,1)S(1)} %slice.145), channel_id=1, source_target_pairs={{0,1},{1,0},{2,3},{3,2},{4,5},{5,4},{6,7},{7,6},{8,24},{9,25},{10,... | collective-permute-start | bytes 909320 | tf_op jit(solution)/shard_map/ppermute | solution.py:683
  39.4 10.3 %collective-permute-start.8 = (bf16[1216,128]{1,0:T(8,128)(2,1)S(1)}, bf16[1216,128]{1,0:T(8,128)(2,1)S(1)}, u32[]{:S(2)}, u32[]{:S(2)}) collective-permute-start(bf16[1216,128]{1,0:T(8,128)(2,1)S(1)} %reduce-precision_convert_fusion.7), channel_id=1, source_target_pairs={{0,16},{1,17},{2,18},{3,19},{4,20},{5,21},{6,22},{7,23},{8,10},{9,... | collective-permute-start | bytes 933896 | tf_op jit(solution)/shard_map/ppermute | solution.py:683
  44.5 15.9 %collective-permute-start.12 = (bf16[1184,128]{1,0:T(8,128)(2,1)S(1)}, bf16[1184,128]{1,0:T(8,128)(2,1)S(1)}, u32[]{:S(2)}, u32[]{:S(2)}) collective-permute-start(bf16[1184,128]{1,0:T(8,128)(2,1)S(1)} %slice.146), channel_id=1, source_target_pairs={{0,16},{1,17},{2,18},{3,19},{4,20},{5,21},{6,22},{7,23},{8,24},{9,... | collective-permute-start | bytes 909320 | tf_op jit(solution)/shard_map/ppermute | solution.py:683
  46.7 13.1 %collective-permute-start.13 = (bf16[1216,128]{1,0:T(8,128)(2,1)S(1)}, bf16[1216,128]{1,0:T(8,128)(2,1)S(1)}, u32[]{:S(2)}, u32[]{:S(2)}) collective-permute-start(bf16[1216,128]{1,0:T(8,128)(2,1)S(1)} %reduce-precision_convert_fusion.6), channel_id=1, source_target_pairs={{0,16},{1,17},{2,18},{3,19},{4,20},{5,21},{6,22},{7,23},{8,10},{9,... | collective-permute-start | bytes 933896 | tf_op jit(solution)/shard_map/ppermute | solution.py:683
  49.9 6.2 %collective-permute-start.10 = (bf16[608,128]{1,0:T(8,128)(2,1)S(1)}, bf16[608,128]{1,0:T(8,128)(2,1)S(1)}, u32[]{:S(2)}, u32[]{:S(2)}) collective-permute-start(bf16[608,128]{1,0:T(8,128)(2,1)S(1)} %slice.149), channel_id=1, source_target_pairs={{0,1},{1,0},{2,3},{3,2},{4,5},{5,4},{6,7},{7,6},{8,24},{9,25},{10,... | collective-permute-start | bytes 466952 | tf_op jit(solution)/shard_map/ppermute | solution.py:683
  52.4 27.3 %collective-permute-start.22 = (bf16[2,288,128]{2,1,0:T(8,128)(2,1)S(1)}, bf16[2,288,128]{2,1,0:T(8,128)(2,1)S(1)}, u32[]{:S(2)}, u32[]{:S(2)}) collective-permute-start(bf16[2,288,128]{2,1,0:T(8,128)(2,1)S(1)} %get-tuple-element.181), channel_id=1, source_target_pairs={{0,8},{1,9},{2,10},{3,11},{4,12},{5,13},{6,14},{7,15},{8,0},{9,1},... | collective-permute-start | bytes 442376 | tf_op jit(solution)/shard_map/ppermute | solution.py:683
  52.9 12.0 %collective-permute-start.9 = (bf16[592,128]{1,0:T(8,128)(2,1)S(1)}, bf16[592,128]{1,0:T(8,128)(2,1)S(1)}, u32[]{:S(2)}, u32[]{:S(2)}) collective-permute-start(bf16[592,128]{1,0:T(8,128)(2,1)S(1)} %reduce-precision_convert_fusion.15), channel_id=1, source_target_pairs={{0,4},{1,5},{2,6},{3,7},{4,0},{5,1},{6,2},{7,3},{8,12},{9,13},{10,... | collective-permute-start | bytes 454664 | tf_op jit(solution)/shard_map/ppermute | solution.py:683
  56.1 6.1 %collective-permute-start.11 = (bf16[304,128]{1,0:T(8,128)(2,1)S(1)}, bf16[304,128]{1,0:T(8,128)(2,1)S(1)}, u32[]{:S(2)}, u32[]{:S(2)}) collective-permute-start(bf16[304,128]{1,0:T(8,128)(2,1)S(1)} %slice.152), channel_id=1, source_target_pairs={{0,2},{1,3},{2,0},{3,1},{4,6},{5,7},{6,4},{7,5},{8,9},{9,8},{10,11... | collective-permute-start | bytes 233480 | tf_op jit(solution)/shard_map/ppermute | solution.py:683
  59.9 9.2 %collective-permute-start.16 = (bf16[608,128]{1,0:T(8,128)(2,1)S(1)}, bf16[608,128]{1,0:T(8,128)(2,1)S(1)}, u32[]{:S(2)}, u32[]{:S(2)}) collective-permute-start(bf16[608,128]{1,0:T(8,128)(2,1)S(1)} %slice.154), channel_id=1, source_target_pairs={{0,1},{1,0},{2,3},{3,2},{4,5},{5,4},{6,7},{7,6},{8,24},{9,25},{10,... | collective-permute-start | bytes 466952 | tf_op jit(solution)/shard_map/ppermute | solution.py:683
  60.5 5.9 %collective-permute-start.17 = (bf16[592,128]{1,0:T(8,128)(2,1)S(1)}, bf16[592,128]{1,0:T(8,128)(2,1)S(1)}, u32[]{:S(2)}, u32[]{:S(2)}) collective-permute-start(bf16[592,128]{1,0:T(8,128)(2,1)S(1)} %slice.155), channel_id=1, source_target_pairs={{0,2},{1,3},{2,0},{3,1},{4,6},{5,7},{6,4},{7,5},{8,9},{9,8},{10,11... | collective-permute-start | bytes 454664 | tf_op jit(solution)/shard_map/ppermute | solution.py:683
  62.2 9.5 %collective-permute-start.15 = (bf16[304,128]{1,0:T(8,128)(2,1)S(1)}, bf16[304,128]{1,0:T(8,128)(2,1)S(1)}, u32[]{:S(2)}, u32[]{:S(2)}) collective-permute-start(bf16[304,128]{1,0:T(8,128)(2,1)S(1)} %reduce-precision_convert_fusion.19), channel_id=1, source_target_pairs={{0,4},{1,5},{2,6},{3,7},{4,0},{5,1},{6,2},{7,3},{8,12},{9,13},{10,... | collective-permute-start | bytes 233480 | tf_op jit(solution)/shard_map/ppermute | solution.py:683
  65.0 6.9 %collective-permute-start.14 = (bf16[592,128]{1,0:T(8,128)(2,1)S(1)}, bf16[592,128]{1,0:T(8,128)(2,1)S(1)}, u32[]{:S(2)}, u32[]{:S(2)}) collective-permute-start(bf16[592,128]{1,0:T(8,128)(2,1)S(1)} %reduce-precision_convert_fusion.14), channel_id=1, source_target_pairs={{0,2},{1,3},{2,0},{3,1},{4,6},{5,7},{6,4},{7,5},{8,9},{9,8},{10,11... | collective-permute-start | bytes 454664 | tf_op jit(solution)/shard_map/ppermute | solution.py:683
  66.5 11.7 %collective-permute-start.23 = (bf16[592,128]{1,0:T(8,128)(2,1)S(1)}, bf16[592,128]{1,0:T(8,128)(2,1)S(1)}, u32[]{:S(2)}, u32[]{:S(2)}) collective-permute-start(bf16[592,128]{1,0:T(8,128)(2,1)S(1)} %reduce-precision_convert_fusion.13), channel_id=1, source_target_pairs={{0,4},{1,5},{2,6},{3,7},{4,0},{5,1},{6,2},{7,3},{8,12},{9,13},{10,... | collective-permute-start | bytes 454664 | tf_op jit(solution)/shard_map/ppermute | solution.py:683
  69.2 7.1 %collective-permute-start.19 = (bf16[304,128]{1,0:T(8,128)(2,1)S(1)}, bf16[304,128]{1,0:T(8,128)(2,1)S(1)}, u32[]{:S(2)}, u32[]{:S(2)}) collective-permute-start(bf16[304,128]{1,0:T(8,128)(2,1)S(1)} %slice.158), channel_id=1, source_target_pairs={{0,2},{1,3},{2,0},{3,1},{4,6},{5,7},{6,4},{7,5},{8,9},{9,8},{10,11... | collective-permute-start | bytes 233480 | tf_op jit(solution)/shard_map/ppermute | solution.py:683
  71.8 9.6 %collective-permute-start.21 = (bf16[304,128]{1,0:T(8,128)(2,1)S(1)}, bf16[304,128]{1,0:T(8,128)(2,1)S(1)}, u32[]{:S(2)}, u32[]{:S(2)}) collective-permute-start(bf16[304,128]{1,0:T(8,128)(2,1)S(1)} %reduce-precision_convert_fusion.18), channel_id=1, source_target_pairs={{0,2},{1,3},{2,0},{3,1},{4,6},{5,7},{6,4},{7,5},{8,9},{9,8},{10,11... | collective-permute-start | bytes 233480 | tf_op jit(solution)/shard_map/ppermute | solution.py:683
  71.9 17.1 %collective-permute-start.18 = (bf16[1184,128]{1,0:T(8,128)(2,1)S(1)}, bf16[1184,128]{1,0:T(8,128)(2,1)S(1)}, u32[]{:S(2)}, u32[]{:S(2)}) collective-permute-start(bf16[1184,128]{1,0:T(8,128)(2,1)S(1)} %pad_maximum_fusion.4), channel_id=1, source_target_pairs={{0,1},{1,0},{2,3},{3,2},{4,5},{5,4},{6,7},{7,6},{8,10},{9,11},{10,... | collective-permute-start | bytes 909320 | tf_op jit(solution)/shard_map/ppermute | solution.py:683
  76.3 6.3 %collective-permute-start.20 = (bf16[304,128]{1,0:T(8,128)(2,1)S(1)}, bf16[304,128]{1,0:T(8,128)(2,1)S(1)}, u32[]{:S(2)}, u32[]{:S(2)}) collective-permute-start(bf16[304,128]{1,0:T(8,128)(2,1)S(1)} %reduce-precision_convert_fusion.17), channel_id=1, source_target_pairs={{0,4},{1,5},{2,6},{3,7},{4,0},{5,1},{6,2},{7,3},{8,12},{9,13},{10,... | collective-permute-start | bytes 233480 | tf_op jit(solution)/shard_map/ppermute | solution.py:683
  78.2 6.8 %collective-permute-start.26 = (bf16[592,128]{1,0:T(8,128)(2,1)S(1)}, bf16[592,128]{1,0:T(8,128)(2,1)S(1)}, u32[]{:S(2)}, u32[]{:S(2)}) collective-permute-start(bf16[592,128]{1,0:T(8,128)(2,1)S(1)} %reduce-precision_convert_fusion.12), channel_id=1, source_target_pairs={{0,2},{1,3},{2,0},{3,1},{4,6},{5,7},{6,4},{7,5},{8,9},{9,8},{10,11... | collective-permute-start | bytes 454664 | tf_op jit(solution)/shard_map/ppermute | solution.py:683
  79.8 9.2 %collective-permute-start.28 = (bf16[4,288,128]{2,1,0:T(8,128)(2,1)S(1)}, bf16[4,288,128]{2,1,0:T(8,128)(2,1)S(1)}, u32[]{:S(2)}, u32[]{:S(2)}) collective-permute-start(bf16[4,288,128]{2,1,0:T(8,128)(2,1)S(1)} %pad_maximum_fusion.6), channel_id=1, source_target_pairs={{0,16},{1,17},{2,18},{3,19},{4,20},{5,21},{6,22},{7,23},{8,24},{9,... | collective-permute-start | bytes 884744 | tf_op jit(solution)/shard_map/ppermute | solution.py:683
  81.4 7.6 %collective-permute-start.27 = (bf16[608,128]{1,0:T(8,128)(2,1)S(1)}, bf16[608,128]{1,0:T(8,128)(2,1)S(1)}, u32[]{:S(2)}, u32[]{:S(2)}) collective-permute-start(bf16[608,128]{1,0:T(8,128)(2,1)S(1)} %pad_maximum_fusion.7), channel_id=1, source_target_pairs={{0,1},{1,0},{2,3},{3,2},{4,5},{5,4},{6,7},{7,6},{8,10},{9,11},{10,... | collective-permute-start | bytes 466952 | tf_op jit(solution)/shard_map/ppermute | solution.py:683
  85.0 8.6 %collective-permute-start.29 = (bf16[1184,128]{1,0:T(8,128)(2,1)S(1)}, bf16[1184,128]{1,0:T(8,128)(2,1)S(1)}, u32[]{:S(2)}, u32[]{:S(2)}) collective-permute-start(bf16[1184,128]{1,0:T(8,128)(2,1)S(1)} %pad_maximum_fusion.5), channel_id=1, source_target_pairs={{0,1},{1,0},{2,3},{3,2},{4,5},{5,4},{6,7},{7,6},{8,10},{9,11},{10,... | collective-permute-start | bytes 909320 | tf_op jit(solution)/shard_map/ppermute | solution.py:683
  (11 other events, 55.6 us)
where the time goes:
time: 96.3 us; the launch traced here: 96.1 us
  starting transfers between devices  40.9 us (42%)
  Pallas kernels  36.1 us (37%)
  waiting for transfers between devices  14.8 us (15%)
  other arithmetic  1.97 us (2%)
  between operations  1.24 us (1%)
  local copies, waits for them, and re-layouts  1.01 us (1%)
    ppermute x31, starting transfers between devices, swap(): return lax.ppermute(value, ('section', 'dp'), route)  40.9 us
    pallas_call x9, Pallas kernels, call(): pl.pallas_call(body, name=name, out_shape=tuple((jax.ShapeDtypeStruct(sha...  36.1 us
    ppermute x31, waiting for transfers between devices, swap(): return lax.ppermute(value, ('section', 'dp'), route)  14.8 us
  transfers between devices with their start and end apart: 31, of which 11 were waited for; matrix products, arithmetic and copies ran while one was open for 2% of the time, Pallas kernels for 19%

commit v1 on v0

--- a/solution.py
+++ b/solution.py
@@ -13,12 +13,18 @@
 VMEM_MIB = {"front": 26, "finish": 20}
 CHOICES = (0, 0, 1, 0)
 PLAN = (
-    "A later_core later_attend A expand core",
-    "C B A C B attend",
-    "D C D A B output R",
-    "A B D C B A C D B",
-    "A D C R B D C R D A",
-    "C B D A B R early C D",
+    "A later_core later_attend A",
+    "expand core C B",
+    "A C B attend",
+    "D C D A",
+    "B output R A",
+    "B D C B",
+    "A C D B",
+    "A D C R",
+    "B D C R",
+    "D A C B",
+    "D A B R",
+    "early C D",
 )
 X_AXIS = -1
 

time: 96.3 us -> 96.3 us (level)
  no operation moved by 1% of the time
where the time goes in v1:
time: 96.3 us; the launch traced here: 96.1 us
  starting transfers between devices  40.9 us (42%)
  Pallas kernels  36.1 us (37%)
  waiting for transfers between devices  14.8 us (15%)
  other arithmetic  1.97 us (2%)
  between operations  1.24 us (1%)
  local copies, waits for them, and re-layouts  1.01 us (1%)
    ppermute x31, starting transfers between devices, swap(): return lax.ppermute(value, ('section', 'dp'), route)  40.9 us
    pallas_call x9, Pallas kernels, call(): pl.pallas_call(body, name=name, out_shape=tuple((jax.ShapeDtypeStruct(sha...  36.1 us
    ppermute x31, waiting for transfers between devices, swap(): return lax.ppermute(value, ('section', 'dp'), route)  14.8 us
  transfers between devices with their start and end apart: 31, of which 11 were waited for; matrix products, arithmetic and copies ran while one was open for 2% of the time, Pallas kernels for 19%

profile of v1, /device:TPU:0, one launch (start us, length us, event | category | flops | bytes accessed | tf_op | source)
XLA Modules:
  0.0 96.1 jit_solution(11823118583616467002)
XLA Ops:
  1.3 16.0 %front.1 = (bf16[384,384]{1,0:T(8,128)(2,1)S(1)}, bf16[384,384]{1,0:T(8,128)(2,1)S(1)}, bf16[384,384]{1,0:T(8,128)(2,1)S(1)}, bf16[384,384]{1,0:T(8,128)(2,1)S(1...) custom-call(bf16[2,197,2,384]{3,2,1,0:T(2,128)(2,1)} %bitcast.12, ...), custom_call_target="tpu_custom_call" | custom-call | flops 8589934592 | bytes 1048576 | tf_op jit(solution)/shard_map/front/pallas_call | solution.py:662
  17.8 2.8 %later_core.1.refs_4_ = bf16[384,1152]{1,0:T(8,128)(2,1)S(1)} custom-call(bf16[384,384]{1,0:T(8,128)(2,1)S(1)} %get-tuple-element.122.refs_0_.refs_2_, bf16[384,384]{1,0:T(8,128)(2,1)S(1)} %get-tuple-element.124.refs_1_, bf16[384,1152]{1,0:T(8,128)(2,1)S(1)} %get-tuple-element.125.refs_2_, f32[16,256]{1,0:T(8,128)S(1)} %get-tuple-element.126.refs_3_), custom_call_target="tpu_custom_call" | custom-call | flops 4294967296 | bytes 1048576 | tf_op jit(solution)/shard_map/later_core/pallas_call | solution.py:662
  20.6 2.0 %later_attend.1 = (bf16[384,384]{1,0:T(8,128)(2,1)S(1)}, bf16[2432,128]{1,0:T(8,128)(2,1)S(1)}, bf16[2432,128]{1,0:T(8,128)(2,1)S(1)}) custom-call(bf16[384,384]{1,0:T(8,128)(2,1)S(1)} %get-tuple-element.120.refs_0_, bf16[384,384]{1,0:T(8,128)(2,1)S(1)} %get-tuple-element.121.refs_1_, bf16[384,384]{1,0:T(8,128)(2,1)S(1)} %get-tuple-element.122.refs_0_.refs_2_, ...), custom_call_target="tpu_custom_call" | custom-call | flops 4294967296 | bytes 1048576 | tf_op jit(solution)/shard_map/later_attend/pallas_call | solution.py:662
  22.8 2.6 %collective-permute-start.1 = (bf16[2368,128]{1,0:T(8,128)(2,1)S(1)}, bf16[2368,128]{1,0:T(8,128)(2,1)S(1)}, u32[]{:S(2)}, u32[]{:S(2)}) collective-permute-start(bf16[2368,128]{1,0:T(8,128)(2,1)S(1)} %reduce-precision_convert_fusion.3), channel_id=1, source_target_pairs={{0,16},{1,17},{2,18},{3,19},{4,20},{5,21},{6,22},{7,23},{8,10},{9,... | collective-permute-start | bytes 1818632 | tf_op jit(solution)/shard_map/ppermute | solution.py:689
  25.4 4.0 %expand_back.1 = (bf16[384,384]{1,0:T(8,128)(2,1)S(1)}, bf16[4736,128]{1,0:T(8,128)(2,1)S(1)}, bf16[4736,128]{1,0:T(8,128)(2,1)S(1)}) custom-call(bf16[384,384]{1,0:T(8,128)(2,1)S(1)} %get-tuple-element.132.refs_0_, bf16[384,384]{1,0:T(8,128)(2,1)S(1)} %get-tuple-element.133.refs_1_, bf16[384,384]{1,0:T(8,128)(2,1)S(1)} %get-tuple-element.134.refs_2_, ...), custom_call_target="tpu_custom_call" | custom-call | flops 4294967296 | bytes 1048576 | tf_op jit(solution)/shard_map/expand_back/pallas_call | solution.py:662
  29.9 2.8 %attend_core.1.refs_4_ = bf16[384,1152]{1,0:T(8,128)(2,1)S(1)} custom-call(bf16[384,384]{1,0:T(8,128)(2,1)S(1)} %get-tuple-element.141.refs_0_.refs_2_, bf16[384,384]{1,0:T(8,128)(2,1)S(1)} %get-tuple-element.142.refs_1_, bf16[384,1152]{1,0:T(8,128)(2,1)S(1)} %get-tuple-element.143.refs_2_, f32[16,256]{1,0:T(8,128)S(1)} %get-tuple-element.144.refs_3_), custom_call_target="tpu_custom_call" | custom-call | flops 4294967296 | bytes 1048576 | tf_op jit(solution)/shard_map/attend_core/pallas_call | solution.py:662
  34.1 2.1 %collective-permute-start.6 = (bf16[2368,128]{1,0:T(8,128)(2,1)S(1)}, bf16[2368,128]{1,0:T(8,128)(2,1)S(1)}, u32[]{:S(2)}, u32[]{:S(2)}) collective-permute-start(bf16[2368,128]{1,0:T(8,128)(2,1)S(1)} %reduce-precision_convert_fusion.1), channel_id=1, source_target_pairs={{0,1},{1,0},{2,3},{3,2},{4,5},{5,4},{6,7},{7,6},{8,10},{9,11},{10,... | collective-permute-start | bytes 1818632 | tf_op jit(solution)/shard_map/ppermute | solution.py:689
  36.3 2.2 %attend_back.1 = (bf16[2,288,128]{2,1,0:T(8,128)(2,1)S(1)}, bf16[2,288,128]{2,1,0:T(8,128)(2,1)S(1)}, bf16[2432,128]{1,0:T(8,128)(2,1)S(1)}, bf16[2432,128]{1,0:T(8,128)(2,1)S(1)}) custom-call(bf16[384,384]{1,0:T(8,128)(2,1)S(1)} %get-tuple-element.146.refs_0_, bf16[384,384]{1,0:T(8,128)(2,1)S(1)} %get-tuple-element.147.refs_1_, ...), custom_call_target="tpu_custom_call" | custom-call | flops 4294967296 | bytes 1048576 | tf_op jit(solution)/shard_map/attend_back/pallas_call | solution.py:662
  41.6 2.6 %collective-permute-done.6 = bf16[2368,128]{1,0:T(8,128)(2,1)S(1)} collective-permute-done((bf16[2368,128]{1,0:T(8,128)(2,1)S(1)}, bf16[2368,128]{1,0:T(8,128)(2,1)S(1)}, u32[]{:S(2)}, u32[]{:S(2)}) %collective-permute-start.6) | collective-permute-done | bytes 606240 | tf_op jit(solution)/shard_map/ppermute | solution.py:689
  44.5 2.1 %collective-permute-start.12 = (bf16[1184,128]{1,0:T(8,128)(2,1)S(1)}, bf16[1184,128]{1,0:T(8,128)(2,1)S(1)}, u32[]{:S(2)}, u32[]{:S(2)}) collective-permute-start(bf16[1184,128]{1,0:T(8,128)(2,1)S(1)} %slice.146), channel_id=1, source_target_pairs={{0,16},{1,17},{2,18},{3,19},{4,20},{5,21},{6,22},{7,23},{8,24},{9,... | collective-permute-start | bytes 909320 | tf_op jit(solution)/shard_map/ppermute | solution.py:689
  47.6 2.1 %collective-permute-start.7 = (bf16[592,128]{1,0:T(8,128)(2,1)S(1)}, bf16[592,128]{1,0:T(8,128)(2,1)S(1)}, u32[]{:S(2)}, u32[]{:S(2)}) collective-permute-start(bf16[592,128]{1,0:T(8,128)(2,1)S(1)} %slice.148), channel_id=1, source_target_pairs={{0,2},{1,3},{2,0},{3,1},{4,6},{5,7},{6,4},{7,5},{8,9},{9,8},{10,11... | collective-permute-start | bytes 454664 | tf_op jit(solution)/shard_map/ppermute | solution.py:689
  52.9 3.1 %collective-permute-start.9 = (bf16[592,128]{1,0:T(8,128)(2,1)S(1)}, bf16[592,128]{1,0:T(8,128)(2,1)S(1)}, u32[]{:S(2)}, u32[]{:S(2)}) collective-permute-start(bf16[592,128]{1,0:T(8,128)(2,1)S(1)} %reduce-precision_convert_fusion.15), channel_id=1, source_target_pairs={{0,4},{1,5},{2,6},{3,7},{4,0},{5,1},{6,2},{7,3},{8,12},{9,13},{10,... | collective-permute-start | bytes 454664 | tf_op jit(solution)/shard_map/ppermute | solution.py:689
  56.1 1.7 %collective-permute-start.11 = (bf16[304,128]{1,0:T(8,128)(2,1)S(1)}, bf16[304,128]{1,0:T(8,128)(2,1)S(1)}, u32[]{:S(2)}, u32[]{:S(2)}) collective-permute-start(bf16[304,128]{1,0:T(8,128)(2,1)S(1)} %slice.152), channel_id=1, source_target_pairs={{0,2},{1,3},{2,0},{3,1},{4,6},{5,7},{6,4},{7,5},{8,9},{9,8},{10,11... | collective-permute-start | bytes 233480 | tf_op jit(solution)/shard_map/ppermute | solution.py:689
  57.7 2.0 %collective-permute-done.13 = bf16[1216,128]{1,0:T(8,128)(2,1)S(1)} collective-permute-done((bf16[1216,128]{1,0:T(8,128)(2,1)S(1)}, bf16[1216,128]{1,0:T(8,128)(2,1)S(1)}, u32[]{:S(2)}, u32[]{:S(2)}) %collective-permute-start.13) | collective-permute-done | bytes 311328 | tf_op jit(solution)/shard_map/ppermute | solution.py:689
  60.5 1.7 %collective-permute-start.17 = (bf16[592,128]{1,0:T(8,128)(2,1)S(1)}, bf16[592,128]{1,0:T(8,128)(2,1)S(1)}, u32[]{:S(2)}, u32[]{:S(2)}) collective-permute-start(bf16[592,128]{1,0:T(8,128)(2,1)S(1)} %slice.155), channel_id=1, source_target_pairs={{0,2},{1,3},{2,0},{3,1},{4,6},{5,7},{6,4},{7,5},{8,9},{9,8},{10,11... | collective-permute-start | bytes 454664 | tf_op jit(solution)/shard_map/ppermute | solution.py:689
  62.2 2.7 %collective-permute-start.15 = (bf16[304,128]{1,0:T(8,128)(2,1)S(1)}, bf16[304,128]{1,0:T(8,128)(2,1)S(1)}, u32[]{:S(2)}, u32[]{:S(2)}) collective-permute-start(bf16[304,128]{1,0:T(8,128)(2,1)S(1)} %reduce-precision_convert_fusion.19), channel_id=1, source_target_pairs={{0,4},{1,5},{2,6},{3,7},{4,0},{5,1},{6,2},{7,3},{8,12},{9,13},{10,... | collective-permute-start | bytes 233480 | tf_op jit(solution)/shard_map/ppermute | solution.py:689
  66.5 2.6 %collective-permute-start.23 = (bf16[592,128]{1,0:T(8,128)(2,1)S(1)}, bf16[592,128]{1,0:T(8,128)(2,1)S(1)}, u32[]{:S(2)}, u32[]{:S(2)}) collective-permute-start(bf16[592,128]{1,0:T(8,128)(2,1)S(1)} %reduce-precision_convert_fusion.13), channel_id=1, source_target_pairs={{0,4},{1,5},{2,6},{3,7},{4,0},{5,1},{6,2},{7,3},{8,12},{9,13},{10,... | collective-permute-start | bytes 454664 | tf_op jit(solution)/shard_map/ppermute | solution.py:689
  69.2 2.5 %collective-permute-start.19 = (bf16[304,128]{1,0:T(8,128)(2,1)S(1)}, bf16[304,128]{1,0:T(8,128)(2,1)S(1)}, u32[]{:S(2)}, u32[]{:S(2)}) collective-permute-start(bf16[304,128]{1,0:T(8,128)(2,1)S(1)} %slice.158), channel_id=1, source_target_pairs={{0,2},{1,3},{2,0},{3,1},{4,6},{5,7},{6,4},{7,5},{8,9},{9,8},{10,11... | collective-permute-start | bytes 233480 | tf_op jit(solution)/shard_map/ppermute | solution.py:689
  71.9 2.3 %collective-permute-start.18 = (bf16[1184,128]{1,0:T(8,128)(2,1)S(1)}, bf16[1184,128]{1,0:T(8,128)(2,1)S(1)}, u32[]{:S(2)}, u32[]{:S(2)}) collective-permute-start(bf16[1184,128]{1,0:T(8,128)(2,1)S(1)} %pad_maximum_fusion.4), channel_id=1, source_target_pairs={{0,1},{1,0},{2,3},{3,2},{4,5},{5,4},{6,7},{7,6},{8,10},{9,11},{10,... | collective-permute-start | bytes 909320 | tf_op jit(solution)/shard_map/ppermute | solution.py:689
  74.2 2.1 %collective-permute-done.19 = bf16[304,128]{1,0:T(8,128)(2,1)S(1)} collective-permute-done((bf16[304,128]{1,0:T(8,128)(2,1)S(1)}, bf16[304,128]{1,0:T(8,128)(2,1)S(1)}, u32[]{:S(2)}, u32[]{:S(2)}) %collective-permute-start.19) | collective-permute-done | bytes 77856 | tf_op jit(solution)/shard_map/ppermute | solution.py:689
  76.3 1.9 %collective-permute-start.20 = (bf16[304,128]{1,0:T(8,128)(2,1)S(1)}, bf16[304,128]{1,0:T(8,128)(2,1)S(1)}, u32[]{:S(2)}, u32[]{:S(2)}) collective-permute-start(bf16[304,128]{1,0:T(8,128)(2,1)S(1)} %reduce-precision_convert_fusion.17), channel_id=1, source_target_pairs={{0,4},{1,5},{2,6},{3,7},{4,0},{5,1},{6,2},{7,3},{8,12},{9,13},{10,... | collective-permute-start | bytes 233480 | tf_op jit(solution)/shard_map/ppermute | solution.py:689
  79.8 1.6 %collective-permute-start.28 = (bf16[4,288,128]{2,1,0:T(8,128)(2,1)S(1)}, bf16[4,288,128]{2,1,0:T(8,128)(2,1)S(1)}, u32[]{:S(2)}, u32[]{:S(2)}) collective-permute-start(bf16[4,288,128]{2,1,0:T(8,128)(2,1)S(1)} %pad_maximum_fusion.6), channel_id=1, source_target_pairs={{0,16},{1,17},{2,18},{3,19},{4,20},{5,21},{6,22},{7,23},{8,24},{9,... | collective-permute-start | bytes 884744 | tf_op jit(solution)/shard_map/ppermute | solution.py:689
  89.1 3.2 %early.1 = (f32[4,96,197]{2,1,0:T(8,128)}, f32[10,37,2,96]{3,2,1,0:T(2,128)}, f32[4,96,197]{2,1,0:T(8,128)}, f32[10,37,2,96]{3,2,1,0:T(2,128)}, f32[2,96,1152]{2...) custom-call(bf16[2368,128]{1,0:T(8,128)(2,1)S(1)} %pad_maximum_fusio, ...), custom_call_target="tpu_custom_call" | custom-call | flops 268435456 | bytes 1048576 | tf_op jit(solution)/shard_map/early/pallas_call | solution.py:662
  93.7 2.3 %finish.1 = (f32[1,96]{1,0:T(1,128)}, f32[2,96]{1,0:T(2,128)}, f32[2,96]{1,0:T(2,128)}, f32[2,192]{1,0:T(2,128)}, f32[2,96]{1,0:T(2,128)}, /*index=5*/f32[2,96]{...) custom-call(bf16[2368,128]{1,0:T(8,128)(2,1)S(1)} %pad_maximum_fusio, ...), custom_call_target="tpu_custom_call", output_to_operand_aliasing={{9}: (3, {}), {10}: (4, {}), {11}: (5, {}), {12}: (6, {})} | custom-call | flops 268435456 | bytes 1048576 | tf_op jit(solution)/shard_map/finish/pallas_call | solution.py:662
  (95 shorter events, 24.0 us)
Async XLA Ops:
  22.8 10.6 %collective-permute-start.1 = (bf16[2368,128]{1,0:T(8,128)(2,1)S(1)}, bf16[2368,128]{1,0:T(8,128)(2,1)S(1)}, u32[]{:S(2)}, u32[]{:S(2)}) collective-permute-start(bf16[2368,128]{1,0:T(8,128)(2,1)S(1)} %reduce-precision_convert_fusion.3), channel_id=1, source_target_pairs={{0,16},{1,17},{2,18},{3,19},{4,20},{5,21},{6,22},{7,23},{8,10},{9,... | collective-permute-start | bytes 1818632 | tf_op jit(solution)/shard_map/ppermute | solution.py:689
  29.7 6.5 %collective-permute-start.3 = (bf16[2432,128]{1,0:T(8,128)(2,1)S(1)}, bf16[2432,128]{1,0:T(8,128)(2,1)S(1)}, u32[]{:S(2)}, u32[]{:S(2)}) collective-permute-start(bf16[2432,128]{1,0:T(8,128)(2,1)S(1)} %get-tuple-element.150), channel_id=1, source_target_pairs={{0,8},{1,9},{2,10},{3,11},{4,12},{5,13},{6,14},{7,15},{8,0},{9,1},... | collective-permute-start | bytes 1867784 | tf_op jit(solution)/shard_map/ppermute | solution.py:689
  34.1 10.1 %collective-permute-start.6 = (bf16[2368,128]{1,0:T(8,128)(2,1)S(1)}, bf16[2368,128]{1,0:T(8,128)(2,1)S(1)}, u32[]{:S(2)}, u32[]{:S(2)}) collective-permute-start(bf16[2368,128]{1,0:T(8,128)(2,1)S(1)} %reduce-precision_convert_fusion.1), channel_id=1, source_target_pairs={{0,1},{1,0},{2,3},{3,2},{4,5},{5,4},{6,7},{7,6},{8,10},{9,11},{10,... | collective-permute-start | bytes 1818632 | tf_op jit(solution)/shard_map/ppermute | solution.py:689
  38.6 8.9 %collective-permute-start.2 = (bf16[1184,128]{1,0:T(8,128)(2,1)S(1)}, bf16[1184,128]{1,0:T(8,128)(2,1)S(1)}, u32[]{:S(2)}, u32[]{:S(2)}) collective-permute-start(bf16[1184,128]{1,0:T(8,128)(2,1)S(1)} %slice.145), channel_id=1, source_target_pairs={{0,1},{1,0},{2,3},{3,2},{4,5},{5,4},{6,7},{7,6},{8,24},{9,25},{10,... | collective-permute-start | bytes 909320 | tf_op jit(solution)/shard_map/ppermute | solution.py:689
  39.4 10.3 %collective-permute-start.8 = (bf16[1216,128]{1,0:T(8,128)(2,1)S(1)}, bf16[1216,128]{1,0:T(8,128)(2,1)S(1)}, u32[]{:S(2)}, u32[]{:S(2)}) collective-permute-start(bf16[1216,128]{1,0:T(8,128)(2,1)S(1)} %reduce-precision_convert_fusion.7), channel_id=1, source_target_pairs={{0,16},{1,17},{2,18},{3,19},{4,20},{5,21},{6,22},{7,23},{8,10},{9,... | collective-permute-start | bytes 933896 | tf_op jit(solution)/shard_map/ppermute | solution.py:689
  44.5 15.9 %collective-permute-start.12 = (bf16[1184,128]{1,0:T(8,128)(2,1)S(1)}, bf16[1184,128]{1,0:T(8,128)(2,1)S(1)}, u32[]{:S(2)}, u32[]{:S(2)}) collective-permute-start(bf16[1184,128]{1,0:T(8,128)(2,1)S(1)} %slice.146), channel_id=1, source_target_pairs={{0,16},{1,17},{2,18},{3,19},{4,20},{5,21},{6,22},{7,23},{8,24},{9,... | collective-permute-start | bytes 909320 | tf_op jit(solution)/shard_map/ppermute | solution.py:689
  46.7 13.1 %collective-permute-start.13 = (bf16[1216,128]{1,0:T(8,128)(2,1)S(1)}, bf16[1216,128]{1,0:T(8,128)(2,1)S(1)}, u32[]{:S(2)}, u32[]{:S(2)}) collective-permute-start(bf16[1216,128]{1,0:T(8,128)(2,1)S(1)} %reduce-precision_convert_fusion.6), channel_id=1, source_target_pairs={{0,16},{1,17},{2,18},{3,19},{4,20},{5,21},{6,22},{7,23},{8,10},{9,... | collective-permute-start | bytes 933896 | tf_op jit(solution)/shard_map/ppermute | solution.py:689
  49.9 6.2 %collective-permute-start.10 = (bf16[608,128]{1,0:T(8,128)(2,1)S(1)}, bf16[608,128]{1,0:T(8,128)(2,1)S(1)}, u32[]{:S(2)}, u32[]{:S(2)}) collective-permute-start(bf16[608,128]{1,0:T(8,128)(2,1)S(1)} %slice.149), channel_id=1, source_target_pairs={{0,1},{1,0},{2,3},{3,2},{4,5},{5,4},{6,7},{7,6},{8,24},{9,25},{10,... | collective-permute-start | bytes 466952 | tf_op jit(solution)/shard_map/ppermute | solution.py:689
  52.4 27.3 %collective-permute-start.22 = (bf16[2,288,128]{2,1,0:T(8,128)(2,1)S(1)}, bf16[2,288,128]{2,1,0:T(8,128)(2,1)S(1)}, u32[]{:S(2)}, u32[]{:S(2)}) collective-permute-start(bf16[2,288,128]{2,1,0:T(8,128)(2,1)S(1)} %get-tuple-element.181), channel_id=1, source_target_pairs={{0,8},{1,9},{2,10},{3,11},{4,12},{5,13},{6,14},{7,15},{8,0},{9,1},... | collective-permute-start | bytes 442376 | tf_op jit(solution)/shard_map/ppermute | solution.py:689
  52.9 12.0 %collective-permute-start.9 = (bf16[592,128]{1,0:T(8,128)(2,1)S(1)}, bf16[592,128]{1,0:T(8,128)(2,1)S(1)}, u32[]{:S(2)}, u32[]{:S(2)}) collective-permute-start(bf16[592,128]{1,0:T(8,128)(2,1)S(1)} %reduce-precision_convert_fusion.15), channel_id=1, source_target_pairs={{0,4},{1,5},{2,6},{3,7},{4,0},{5,1},{6,2},{7,3},{8,12},{9,13},{10,... | collective-permute-start | bytes 454664 | tf_op jit(solution)/shard_map/ppermute | solution.py:689
  56.1 6.1 %collective-permute-start.11 = (bf16[304,128]{1,0:T(8,128)(2,1)S(1)}, bf16[304,128]{1,0:T(8,128)(2,1)S(1)}, u32[]{:S(2)}, u32[]{:S(2)}) collective-permute-start(bf16[304,128]{1,0:T(8,128)(2,1)S(1)} %slice.152), channel_id=1, source_target_pairs={{0,2},{1,3},{2,0},{3,1},{4,6},{5,7},{6,4},{7,5},{8,9},{9,8},{10,11... | collective-permute-start | bytes 233480 | tf_op jit(solution)/shard_map/ppermute | solution.py:689
  59.9 9.2 %collective-permute-start.16 = (bf16[608,128]{1,0:T(8,128)(2,1)S(1)}, bf16[608,128]{1,0:T(8,128)(2,1)S(1)}, u32[]{:S(2)}, u32[]{:S(2)}) collective-permute-start(bf16[608,128]{1,0:T(8,128)(2,1)S(1)} %slice.154), channel_id=1, source_target_pairs={{0,1},{1,0},{2,3},{3,2},{4,5},{5,4},{6,7},{7,6},{8,24},{9,25},{10,... | collective-permute-start | bytes 466952 | tf_op jit(solution)/shard_map/ppermute | solution.py:689
  60.5 5.9 %collective-permute-start.17 = (bf16[592,128]{1,0:T(8,128)(2,1)S(1)}, bf16[592,128]{1,0:T(8,128)(2,1)S(1)}, u32[]{:S(2)}, u32[]{:S(2)}) collective-permute-start(bf16[592,128]{1,0:T(8,128)(2,1)S(1)} %slice.155), channel_id=1, source_target_pairs={{0,2},{1,3},{2,0},{3,1},{4,6},{5,7},{6,4},{7,5},{8,9},{9,8},{10,11... | collective-permute-start | bytes 454664 | tf_op jit(solution)/shard_map/ppermute | solution.py:689
  62.2 9.5 %collective-permute-start.15 = (bf16[304,128]{1,0:T(8,128)(2,1)S(1)}, bf16[304,128]{1,0:T(8,128)(2,1)S(1)}, u32[]{:S(2)}, u32[]{:S(2)}) collective-permute-start(bf16[304,128]{1,0:T(8,128)(2,1)S(1)} %reduce-precision_convert_fusion.19), channel_id=1, source_target_pairs={{0,4},{1,5},{2,6},{3,7},{4,0},{5,1},{6,2},{7,3},{8,12},{9,13},{10,... | collective-permute-start | bytes 233480 | tf_op jit(solution)/shard_map/ppermute | solution.py:689
  65.0 6.9 %collective-permute-start.14 = (bf16[592,128]{1,0:T(8,128)(2,1)S(1)}, bf16[592,128]{1,0:T(8,128)(2,1)S(1)}, u32[]{:S(2)}, u32[]{:S(2)}) collective-permute-start(bf16[592,128]{1,0:T(8,128)(2,1)S(1)} %reduce-precision_convert_fusion.14), channel_id=1, source_target_pairs={{0,2},{1,3},{2,0},{3,1},{4,6},{5,7},{6,4},{7,5},{8,9},{9,8},{10,11... | collective-permute-start | bytes 454664 | tf_op jit(solution)/shard_map/ppermute | solution.py:689
  66.5 11.7 %collective-permute-start.23 = (bf16[592,128]{1,0:T(8,128)(2,1)S(1)}, bf16[592,128]{1,0:T(8,128)(2,1)S(1)}, u32[]{:S(2)}, u32[]{:S(2)}) collective-permute-start(bf16[592,128]{1,0:T(8,128)(2,1)S(1)} %reduce-precision_convert_fusion.13), channel_id=1, source_target_pairs={{0,4},{1,5},{2,6},{3,7},{4,0},{5,1},{6,2},{7,3},{8,12},{9,13},{10,... | collective-permute-start | bytes 454664 | tf_op jit(solution)/shard_map/ppermute | solution.py:689
  69.2 7.1 %collective-permute-start.19 = (bf16[304,128]{1,0:T(8,128)(2,1)S(1)}, bf16[304,128]{1,0:T(8,128)(2,1)S(1)}, u32[]{:S(2)}, u32[]{:S(2)}) collective-permute-start(bf16[304,128]{1,0:T(8,128)(2,1)S(1)} %slice.158), channel_id=1, source_target_pairs={{0,2},{1,3},{2,0},{3,1},{4,6},{5,7},{6,4},{7,5},{8,9},{9,8},{10,11... | collective-permute-start | bytes 233480 | tf_op jit(solution)/shard_map/ppermute | solution.py:689
  71.8 9.6 %collective-permute-start.21 = (bf16[304,128]{1,0:T(8,128)(2,1)S(1)}, bf16[304,128]{1,0:T(8,128)(2,1)S(1)}, u32[]{:S(2)}, u32[]{:S(2)}) collective-permute-start(bf16[304,128]{1,0:T(8,128)(2,1)S(1)} %reduce-precision_convert_fusion.18), channel_id=1, source_target_pairs={{0,2},{1,3},{2,0},{3,1},{4,6},{5,7},{6,4},{7,5},{8,9},{9,8},{10,11... | collective-permute-start | bytes 233480 | tf_op jit(solution)/shard_map/ppermute | solution.py:689
  71.9 17.1 %collective-permute-start.18 = (bf16[1184,128]{1,0:T(8,128)(2,1)S(1)}, bf16[1184,128]{1,0:T(8,128)(2,1)S(1)}, u32[]{:S(2)}, u32[]{:S(2)}) collective-permute-start(bf16[1184,128]{1,0:T(8,128)(2,1)S(1)} %pad_maximum_fusion.4), channel_id=1, source_target_pairs={{0,1},{1,0},{2,3},{3,2},{4,5},{5,4},{6,7},{7,6},{8,10},{9,11},{10,... | collective-permute-start | bytes 909320 | tf_op jit(solution)/shard_map/ppermute | solution.py:689
  76.3 6.3 %collective-permute-start.20 = (bf16[304,128]{1,0:T(8,128)(2,1)S(1)}, bf16[304,128]{1,0:T(8,128)(2,1)S(1)}, u32[]{:S(2)}, u32[]{:S(2)}) collective-permute-start(bf16[304,128]{1,0:T(8,128)(2,1)S(1)} %reduce-precision_convert_fusion.17), channel_id=1, source_target_pairs={{0,4},{1,5},{2,6},{3,7},{4,0},{5,1},{6,2},{7,3},{8,12},{9,13},{10,... | collective-permute-start | bytes 233480 | tf_op jit(solution)/shard_map/ppermute | solution.py:689
  78.2 6.8 %collective-permute-start.26 = (bf16[592,128]{1,0:T(8,128)(2,1)S(1)}, bf16[592,128]{1,0:T(8,128)(2,1)S(1)}, u32[]{:S(2)}, u32[]{:S(2)}) collective-permute-start(bf16[592,128]{1,0:T(8,128)(2,1)S(1)} %reduce-precision_convert_fusion.12), channel_id=1, source_target_pairs={{0,2},{1,3},{2,0},{3,1},{4,6},{5,7},{6,4},{7,5},{8,9},{9,8},{10,11... | collective-permute-start | bytes 454664 | tf_op jit(solution)/shard_map/ppermute | solution.py:689
  79.8 9.2 %collective-permute-start.28 = (bf16[4,288,128]{2,1,0:T(8,128)(2,1)S(1)}, bf16[4,288,128]{2,1,0:T(8,128)(2,1)S(1)}, u32[]{:S(2)}, u32[]{:S(2)}) collective-permute-start(bf16[4,288,128]{2,1,0:T(8,128)(2,1)S(1)} %pad_maximum_fusion.6), channel_id=1, source_target_pairs={{0,16},{1,17},{2,18},{3,19},{4,20},{5,21},{6,22},{7,23},{8,24},{9,... | collective-permute-start | bytes 884744 | tf_op jit(solution)/shard_map/ppermute | solution.py:689
  81.4 7.6 %collective-permute-start.27 = (bf16[608,128]{1,0:T(8,128)(2,1)S(1)}, bf16[608,128]{1,0:T(8,128)(2,1)S(1)}, u32[]{:S(2)}, u32[]{:S(2)}) collective-permute-start(bf16[608,128]{1,0:T(8,128)(2,1)S(1)} %pad_maximum_fusion.7), channel_id=1, source_target_pairs={{0,1},{1,0},{2,3},{3,2},{4,5},{5,4},{6,7},{7,6},{8,10},{9,11},{10,... | collective-permute-start | bytes 466952 | tf_op jit(solution)/shard_map/ppermute | solution.py:689
  85.0 8.6 %collective-permute-start.29 = (bf16[1184,128]{1,0:T(8,128)(2,1)S(1)}, bf16[1184,128]{1,0:T(8,128)(2,1)S(1)}, u32[]{:S(2)}, u32[]{:S(2)}) collective-permute-start(bf16[1184,128]{1,0:T(8,128)(2,1)S(1)} %pad_maximum_fusion.5), channel_id=1, source_target_pairs={{0,1},{1,0},{2,3},{3,2},{4,5},{5,4},{6,7},{7,6},{8,10},{9,11},{10,... | collective-permute-start | bytes 909320 | tf_op jit(solution)/shard_map/ppermute | solution.py:689
  (11 other events, 55.6 us)

commit v2 on v1

--- a/solution.py
+++ b/solution.py
@@ -555,14 +555,20 @@
         target[:, tile * LANES : (tile + 1) * LANES] = source[base + tile * r : base + (tile + 1) * r, :].astype(f32)
 
 
-def widen(sz, attend, expand, targets, moves):
-    triple, output, up, down = targets
-    hidden_rows = sz.hidden // LANES * sz.cut
-    for index, (source, base, target) in enumerate(
-        ((expand, 0, up), (expand, hidden_rows, down), (attend, 0, triple), (attend, 3 * sz.tiles * sz.cut, output))
-    ):
-        widen_tiles(source, base, target)
-        moves[(2, 3, 0, 1)[index]].start()
+def widen_expand(sz, source, targets, moves):
+    _, _, up, down = targets
+    widen_tiles(source, 0, up)
+    moves[2].start()
+    widen_tiles(source, sz.hidden // LANES * sz.cut, down)
+    moves[3].start()
+
+
+def widen_attend(sz, source, targets, moves):
+    triple, output, _, _ = targets
+    widen_tiles(source, 0, triple)
+    moves[0].start()
+    widen_tiles(source, 3 * sz.tiles * sz.cut, output)
+    moves[1].start()
 
 
 def early_kernel(sz, *refs):
@@ -572,8 +578,9 @@
     me, replica = lax.axis_index("section"), lax.axis_index("dp")
     moves = [pltpu.make_async_copy(target, out.at[1], sems.at[i]) for i, (target, out) in enumerate(zip(targets, outs))]
     unpack(sz.exchanges["A"], me, replica, expand_in, expand)
+    widen_expand(sz, expand, targets, moves)
     unpack(sz.exchanges["B"], me, replica, attend_in, attend)
-    widen(sz, attend, expand, targets, moves)
+    widen_attend(sz, attend, targets, moves)
     vectors[: sz.small_rows, :] = attend[sz.attend_full : sz.attend_full + sz.small_rows, :].astype(f32)
     vectors[sz.small_rows :, :] = expand[sz.expand_full : sz.expand_full + sz.small_rows, :].astype(f32)
     row_parts = (
@@ -611,8 +618,9 @@
     me, replica = lax.axis_index("section"), lax.axis_index("dp")
     moves = [pltpu.make_async_copy(target, out.at[0], sems.at[i]) for i, (target, out) in enumerate(zip(targets, outs))]
     unpack(sz.exchanges["C"], me, replica, expand_in, expand)
+    widen_expand(sz, expand, targets, moves)
     unpack(sz.exchanges["D"], me, replica, attend_in, attend)
-    widen(sz, attend, expand, targets, moves)
+    widen_attend(sz, attend, targets, moves)
     width, tiles, cut = sz.width, sz.tiles, sz.cut
     row = lax.broadcasted_iota(jnp.int32, (width, cut), 0)
     column = lax.broadcasted_iota(jnp.int32, (width, cut), 1)

time: 96.3 us -> 96.3 us (level)
  no operation moved by 1% of the time
where the time goes in v2:
time: 96.3 us; the launch traced here: 96.1 us
  starting transfers between devices  40.9 us (42%)
  Pallas kernels  36.1 us (37%)
  waiting for transfers between devices  14.8 us (15%)
  other arithmetic  1.97 us (2%)
  between operations  1.24 us (1%)
  local copies, waits for them, and re-layouts  1.01 us (1%)
    ppermute x31, starting transfers between devices, swap(): return lax.ppermute(value, ('section', 'dp'), route)  40.9 us
    pallas_call x9, Pallas kernels, call(): pl.pallas_call(body, name=name, out_shape=tuple((jax.ShapeDtypeStruct(sha...  36.1 us
    ppermute x31, waiting for transfers between devices, swap(): return lax.ppermute(value, ('section', 'dp'), route)  14.8 us
  transfers between devices with their start and end apart: 31, of which 11 were waited for; matrix products, arithmetic and copies ran while one was open for 2% of the time, Pallas kernels for 19%

profile of v2, /device:TPU:0, one launch (start us, length us, event | category | flops | bytes accessed | tf_op | source)
XLA Modules:
  0.0 96.1 jit_solution(11823118583616467002)
XLA Ops:
  1.3 16.0 %front.1 = (bf16[384,384]{1,0:T(8,128)(2,1)S(1)}, bf16[384,384]{1,0:T(8,128)(2,1)S(1)}, bf16[384,384]{1,0:T(8,128)(2,1)S(1)}, bf16[384,384]{1,0:T(8,128)(2,1)S(1...) custom-call(bf16[2,197,2,384]{3,2,1,0:T(2,128)(2,1)} %bitcast.12, ...), custom_call_target="tpu_custom_call" | custom-call | flops 8589934592 | bytes 1048576 | tf_op jit(solution)/shard_map/front/pallas_call | solution.py:670
  17.8 2.8 %later_core.1.refs_4_ = bf16[384,1152]{1,0:T(8,128)(2,1)S(1)} custom-call(bf16[384,384]{1,0:T(8,128)(2,1)S(1)} %get-tuple-element.122.refs_0_.refs_2_, bf16[384,384]{1,0:T(8,128)(2,1)S(1)} %get-tuple-element.124.refs_1_, bf16[384,1152]{1,0:T(8,128)(2,1)S(1)} %get-tuple-element.125.refs_2_, f32[16,256]{1,0:T(8,128)S(1)} %get-tuple-element.126.refs_3_), custom_call_target="tpu_custom_call" | custom-call | flops 4294967296 | bytes 1048576 | tf_op jit(solution)/shard_map/later_core/pallas_call | solution.py:670
  20.6 2.0 %later_attend.1 = (bf16[384,384]{1,0:T(8,128)(2,1)S(1)}, bf16[2432,128]{1,0:T(8,128)(2,1)S(1)}, bf16[2432,128]{1,0:T(8,128)(2,1)S(1)}) custom-call(bf16[384,384]{1,0:T(8,128)(2,1)S(1)} %get-tuple-element.120.refs_0_, bf16[384,384]{1,0:T(8,128)(2,1)S(1)} %get-tuple-element.121.refs_1_, bf16[384,384]{1,0:T(8,128)(2,1)S(1)} %get-tuple-element.122.refs_0_.refs_2_, ...), custom_call_target="tpu_custom_call" | custom-call | flops 4294967296 | bytes 1048576 | tf_op jit(solution)/shard_map/later_attend/pallas_call | solution.py:670
  22.8 2.6 %collective-permute-start.1 = (bf16[2368,128]{1,0:T(8,128)(2,1)S(1)}, bf16[2368,128]{1,0:T(8,128)(2,1)S(1)}, u32[]{:S(2)}, u32[]{:S(2)}) collective-permute-start(bf16[2368,128]{1,0:T(8,128)(2,1)S(1)} %reduce-precision_convert_fusion.3), channel_id=1, source_target_pairs={{0,16},{1,17},{2,18},{3,19},{4,20},{5,21},{6,22},{7,23},{8,10},{9,... | collective-permute-start | bytes 1818632 | tf_op jit(solution)/shard_map/ppermute | solution.py:697
  25.4 4.0 %expand_back.1 = (bf16[384,384]{1,0:T(8,128)(2,1)S(1)}, bf16[4736,128]{1,0:T(8,128)(2,1)S(1)}, bf16[4736,128]{1,0:T(8,128)(2,1)S(1)}) custom-call(bf16[384,384]{1,0:T(8,128)(2,1)S(1)} %get-tuple-element.132.refs_0_, bf16[384,384]{1,0:T(8,128)(2,1)S(1)} %get-tuple-element.133.refs_1_, bf16[384,384]{1,0:T(8,128)(2,1)S(1)} %get-tuple-element.134.refs_2_, ...), custom_call_target="tpu_custom_call" | custom-call | flops 4294967296 | bytes 1048576 | tf_op jit(solution)/shard_map/expand_back/pallas_call | solution.py:670
  29.9 2.8 %attend_core.1.refs_4_ = bf16[384,1152]{1,0:T(8,128)(2,1)S(1)} custom-call(bf16[384,384]{1,0:T(8,128)(2,1)S(1)} %get-tuple-element.141.refs_0_.refs_2_, bf16[384,384]{1,0:T(8,128)(2,1)S(1)} %get-tuple-element.142.refs_1_, bf16[384,1152]{1,0:T(8,128)(2,1)S(1)} %get-tuple-element.143.refs_2_, f32[16,256]{1,0:T(8,128)S(1)} %get-tuple-element.144.refs_3_), custom_call_target="tpu_custom_call" | custom-call | flops 4294967296 | bytes 1048576 | tf_op jit(solution)/shard_map/attend_core/pallas_call | solution.py:670
  34.1 2.1 %collective-permute-start.6 = (bf16[2368,128]{1,0:T(8,128)(2,1)S(1)}, bf16[2368,128]{1,0:T(8,128)(2,1)S(1)}, u32[]{:S(2)}, u32[]{:S(2)}) collective-permute-start(bf16[2368,128]{1,0:T(8,128)(2,1)S(1)} %reduce-precision_convert_fusion.1), channel_id=1, source_target_pairs={{0,1},{1,0},{2,3},{3,2},{4,5},{5,4},{6,7},{7,6},{8,10},{9,11},{10,... | collective-permute-start | bytes 1818632 | tf_op jit(solution)/shard_map/ppermute | solution.py:697
  36.3 2.2 %attend_back.1 = (bf16[2,288,128]{2,1,0:T(8,128)(2,1)S(1)}, bf16[2,288,128]{2,1,0:T(8,128)(2,1)S(1)}, bf16[2432,128]{1,0:T(8,128)(2,1)S(1)}, bf16[2432,128]{1,0:T(8,128)(2,1)S(1)}) custom-call(bf16[384,384]{1,0:T(8,128)(2,1)S(1)} %get-tuple-element.146.refs_0_, bf16[384,384]{1,0:T(8,128)(2,1)S(1)} %get-tuple-element.147.refs_1_, ...), custom_call_target="tpu_custom_call" | custom-call | flops 4294967296 | bytes 1048576 | tf_op jit(solution)/shard_map/attend_back/pallas_call | solution.py:670
  41.6 2.6 %collective-permute-done.6 = bf16[2368,128]{1,0:T(8,128)(2,1)S(1)} collective-permute-done((bf16[2368,128]{1,0:T(8,128)(2,1)S(1)}, bf16[2368,128]{1,0:T(8,128)(2,1)S(1)}, u32[]{:S(2)}, u32[]{:S(2)}) %collective-permute-start.6) | collective-permute-done | bytes 606240 | tf_op jit(solution)/shard_map/ppermute | solution.py:697
  44.5 2.1 %collective-permute-start.12 = (bf16[1184,128]{1,0:T(8,128)(2,1)S(1)}, bf16[1184,128]{1,0:T(8,128)(2,1)S(1)}, u32[]{:S(2)}, u32[]{:S(2)}) collective-permute-start(bf16[1184,128]{1,0:T(8,128)(2,1)S(1)} %slice.146), channel_id=1, source_target_pairs={{0,16},{1,17},{2,18},{3,19},{4,20},{5,21},{6,22},{7,23},{8,24},{9,... | collective-permute-start | bytes 909320 | tf_op jit(solution)/shard_map/ppermute | solution.py:697
  47.6 2.1 %collective-permute-start.7 = (bf16[592,128]{1,0:T(8,128)(2,1)S(1)}, bf16[592,128]{1,0:T(8,128)(2,1)S(1)}, u32[]{:S(2)}, u32[]{:S(2)}) collective-permute-start(bf16[592,128]{1,0:T(8,128)(2,1)S(1)} %slice.148), channel_id=1, source_target_pairs={{0,2},{1,3},{2,0},{3,1},{4,6},{5,7},{6,4},{7,5},{8,9},{9,8},{10,11... | collective-permute-start | bytes 454664 | tf_op jit(solution)/shard_map/ppermute | solution.py:697
  52.9 3.1 %collective-permute-start.9 = (bf16[592,128]{1,0:T(8,128)(2,1)S(1)}, bf16[592,128]{1,0:T(8,128)(2,1)S(1)}, u32[]{:S(2)}, u32[]{:S(2)}) collective-permute-start(bf16[592,128]{1,0:T(8,128)(2,1)S(1)} %reduce-precision_convert_fusion.15), channel_id=1, source_target_pairs={{0,4},{1,5},{2,6},{3,7},{4,0},{5,1},{6,2},{7,3},{8,12},{9,13},{10,... | collective-permute-start | bytes 454664 | tf_op jit(solution)/shard_map/ppermute | solution.py:697
  56.1 1.7 %collective-permute-start.11 = (bf16[304,128]{1,0:T(8,128)(2,1)S(1)}, bf16[304,128]{1,0:T(8,128)(2,1)S(1)}, u32[]{:S(2)}, u32[]{:S(2)}) collective-permute-start(bf16[304,128]{1,0:T(8,128)(2,1)S(1)} %slice.152), channel_id=1, source_target_pairs={{0,2},{1,3},{2,0},{3,1},{4,6},{5,7},{6,4},{7,5},{8,9},{9,8},{10,11... | collective-permute-start | bytes 233480 | tf_op jit(solution)/shard_map/ppermute | solution.py:697
  57.7 2.0 %collective-permute-done.13 = bf16[1216,128]{1,0:T(8,128)(2,1)S(1)} collective-permute-done((bf16[1216,128]{1,0:T(8,128)(2,1)S(1)}, bf16[1216,128]{1,0:T(8,128)(2,1)S(1)}, u32[]{:S(2)}, u32[]{:S(2)}) %collective-permute-start.13) | collective-permute-done | bytes 311328 | tf_op jit(solution)/shard_map/ppermute | solution.py:697
  60.5 1.7 %collective-permute-start.17 = (bf16[592,128]{1,0:T(8,128)(2,1)S(1)}, bf16[592,128]{1,0:T(8,128)(2,1)S(1)}, u32[]{:S(2)}, u32[]{:S(2)}) collective-permute-start(bf16[592,128]{1,0:T(8,128)(2,1)S(1)} %slice.155), channel_id=1, source_target_pairs={{0,2},{1,3},{2,0},{3,1},{4,6},{5,7},{6,4},{7,5},{8,9},{9,8},{10,11... | collective-permute-start | bytes 454664 | tf_op jit(solution)/shard_map/ppermute | solution.py:697
  62.2 2.7 %collective-permute-start.15 = (bf16[304,128]{1,0:T(8,128)(2,1)S(1)}, bf16[304,128]{1,0:T(8,128)(2,1)S(1)}, u32[]{:S(2)}, u32[]{:S(2)}) collective-permute-start(bf16[304,128]{1,0:T(8,128)(2,1)S(1)} %reduce-precision_convert_fusion.19), channel_id=1, source_target_pairs={{0,4},{1,5},{2,6},{3,7},{4,0},{5,1},{6,2},{7,3},{8,12},{9,13},{10,... | collective-permute-start | bytes 233480 | tf_op jit(solution)/shard_map/ppermute | solution.py:697
  66.5 2.6 %collective-permute-start.23 = (bf16[592,128]{1,0:T(8,128)(2,1)S(1)}, bf16[592,128]{1,0:T(8,128)(2,1)S(1)}, u32[]{:S(2)}, u32[]{:S(2)}) collective-permute-start(bf16[592,128]{1,0:T(8,128)(2,1)S(1)} %reduce-precision_convert_fusion.13), channel_id=1, source_target_pairs={{0,4},{1,5},{2,6},{3,7},{4,0},{5,1},{6,2},{7,3},{8,12},{9,13},{10,... | collective-permute-start | bytes 454664 | tf_op jit(solution)/shard_map/ppermute | solution.py:697
  69.2 2.5 %collective-permute-start.19 = (bf16[304,128]{1,0:T(8,128)(2,1)S(1)}, bf16[304,128]{1,0:T(8,128)(2,1)S(1)}, u32[]{:S(2)}, u32[]{:S(2)}) collective-permute-start(bf16[304,128]{1,0:T(8,128)(2,1)S(1)} %slice.158), channel_id=1, source_target_pairs={{0,2},{1,3},{2,0},{3,1},{4,6},{5,7},{6,4},{7,5},{8,9},{9,8},{10,11... | collective-permute-start | bytes 233480 | tf_op jit(solution)/shard_map/ppermute | solution.py:697
  71.9 2.3 %collective-permute-start.18 = (bf16[1184,128]{1,0:T(8,128)(2,1)S(1)}, bf16[1184,128]{1,0:T(8,128)(2,1)S(1)}, u32[]{:S(2)}, u32[]{:S(2)}) collective-permute-start(bf16[1184,128]{1,0:T(8,128)(2,1)S(1)} %pad_maximum_fusion.4), channel_id=1, source_target_pairs={{0,1},{1,0},{2,3},{3,2},{4,5},{5,4},{6,7},{7,6},{8,10},{9,11},{10,... | collective-permute-start | bytes 909320 | tf_op jit(solution)/shard_map/ppermute | solution.py:697
  74.2 2.1 %collective-permute-done.19 = bf16[304,128]{1,0:T(8,128)(2,1)S(1)} collective-permute-done((bf16[304,128]{1,0:T(8,128)(2,1)S(1)}, bf16[304,128]{1,0:T(8,128)(2,1)S(1)}, u32[]{:S(2)}, u32[]{:S(2)}) %collective-permute-start.19) | collective-permute-done | bytes 77856 | tf_op jit(solution)/shard_map/ppermute | solution.py:697
  76.3 1.9 %collective-permute-start.20 = (bf16[304,128]{1,0:T(8,128)(2,1)S(1)}, bf16[304,128]{1,0:T(8,128)(2,1)S(1)}, u32[]{:S(2)}, u32[]{:S(2)}) collective-permute-start(bf16[304,128]{1,0:T(8,128)(2,1)S(1)} %reduce-precision_convert_fusion.17), channel_id=1, source_target_pairs={{0,4},{1,5},{2,6},{3,7},{4,0},{5,1},{6,2},{7,3},{8,12},{9,13},{10,... | collective-permute-start | bytes 233480 | tf_op jit(solution)/shard_map/ppermute | solution.py:697
  79.8 1.6 %collective-permute-start.28 = (bf16[4,288,128]{2,1,0:T(8,128)(2,1)S(1)}, bf16[4,288,128]{2,1,0:T(8,128)(2,1)S(1)}, u32[]{:S(2)}, u32[]{:S(2)}) collective-permute-start(bf16[4,288,128]{2,1,0:T(8,128)(2,1)S(1)} %pad_maximum_fusion.6), channel_id=1, source_target_pairs={{0,16},{1,17},{2,18},{3,19},{4,20},{5,21},{6,22},{7,23},{8,24},{9,... | collective-permute-start | bytes 884744 | tf_op jit(solution)/shard_map/ppermute | solution.py:697
  89.1 3.2 %early.1 = (f32[4,96,197]{2,1,0:T(8,128)}, f32[10,37,2,96]{3,2,1,0:T(2,128)}, f32[4,96,197]{2,1,0:T(8,128)}, f32[10,37,2,96]{3,2,1,0:T(2,128)}, f32[2,96,1152]{2...) custom-call(bf16[2368,128]{1,0:T(8,128)(2,1)S(1)} %pad_maximum_fusio, ...), custom_call_target="tpu_custom_call" | custom-call | flops 268435456 | bytes 1048576 | tf_op jit(solution)/shard_map/early/pallas_call | solution.py:670
  93.7 2.3 %finish.1 = (f32[1,96]{1,0:T(1,128)}, f32[2,96]{1,0:T(2,128)}, f32[2,96]{1,0:T(2,128)}, f32[2,192]{1,0:T(2,128)}, f32[2,96]{1,0:T(2,128)}, /*index=5*/f32[2,96]{...) custom-call(bf16[2368,128]{1,0:T(8,128)(2,1)S(1)} %pad_maximum_fusio, ...), custom_call_target="tpu_custom_call", output_to_operand_aliasing={{9}: (3, {}), {10}: (4, {}), {11}: (5, {}), {12}: (6, {})} | custom-call | flops 268435456 | bytes 1048576 | tf_op jit(solution)/shard_map/finish/pallas_call | solution.py:670
  (95 shorter events, 24.0 us)
Async XLA Ops:
  22.8 10.6 %collective-permute-start.1 = (bf16[2368,128]{1,0:T(8,128)(2,1)S(1)}, bf16[2368,128]{1,0:T(8,128)(2,1)S(1)}, u32[]{:S(2)}, u32[]{:S(2)}) collective-permute-start(bf16[2368,128]{1,0:T(8,128)(2,1)S(1)} %reduce-precision_convert_fusion.3), channel_id=1, source_target_pairs={{0,16},{1,17},{2,18},{3,19},{4,20},{5,21},{6,22},{7,23},{8,10},{9,... | collective-permute-start | bytes 1818632 | tf_op jit(solution)/shard_map/ppermute | solution.py:697
  29.7 6.5 %collective-permute-start.3 = (bf16[2432,128]{1,0:T(8,128)(2,1)S(1)}, bf16[2432,128]{1,0:T(8,128)(2,1)S(1)}, u32[]{:S(2)}, u32[]{:S(2)}) collective-permute-start(bf16[2432,128]{1,0:T(8,128)(2,1)S(1)} %get-tuple-element.150), channel_id=1, source_target_pairs={{0,8},{1,9},{2,10},{3,11},{4,12},{5,13},{6,14},{7,15},{8,0},{9,1},... | collective-permute-start | bytes 1867784 | tf_op jit(solution)/shard_map/ppermute | solution.py:697
  34.1 10.1 %collective-permute-start.6 = (bf16[2368,128]{1,0:T(8,128)(2,1)S(1)}, bf16[2368,128]{1,0:T(8,128)(2,1)S(1)}, u32[]{:S(2)}, u32[]{:S(2)}) collective-permute-start(bf16[2368,128]{1,0:T(8,128)(2,1)S(1)} %reduce-precision_convert_fusion.1), channel_id=1, source_target_pairs={{0,1},{1,0},{2,3},{3,2},{4,5},{5,4},{6,7},{7,6},{8,10},{9,11},{10,... | collective-permute-start | bytes 1818632 | tf_op jit(solution)/shard_map/ppermute | solution.py:697
  38.6 8.9 %collective-permute-start.2 = (bf16[1184,128]{1,0:T(8,128)(2,1)S(1)}, bf16[1184,128]{1,0:T(8,128)(2,1)S(1)}, u32[]{:S(2)}, u32[]{:S(2)}) collective-permute-start(bf16[1184,128]{1,0:T(8,128)(2,1)S(1)} %slice.145), channel_id=1, source_target_pairs={{0,1},{1,0},{2,3},{3,2},{4,5},{5,4},{6,7},{7,6},{8,24},{9,25},{10,... | collective-permute-start | bytes 909320 | tf_op jit(solution)/shard_map/ppermute | solution.py:697
  39.4 10.3 %collective-permute-start.8 = (bf16[1216,128]{1,0:T(8,128)(2,1)S(1)}, bf16[1216,128]{1,0:T(8,128)(2,1)S(1)}, u32[]{:S(2)}, u32[]{:S(2)}) collective-permute-start(bf16[1216,128]{1,0:T(8,128)(2,1)S(1)} %reduce-precision_convert_fusion.7), channel_id=1, source_target_pairs={{0,16},{1,17},{2,18},{3,19},{4,20},{5,21},{6,22},{7,23},{8,10},{9,... | collective-permute-start | bytes 933896 | tf_op jit(solution)/shard_map/ppermute | solution.py:697
  44.5 15.9 %collective-permute-start.12 = (bf16[1184,128]{1,0:T(8,128)(2,1)S(1)}, bf16[1184,128]{1,0:T(8,128)(2,1)S(1)}, u32[]{:S(2)}, u32[]{:S(2)}) collective-permute-start(bf16[1184,128]{1,0:T(8,128)(2,1)S(1)} %slice.146), channel_id=1, source_target_pairs={{0,16},{1,17},{2,18},{3,19},{4,20},{5,21},{6,22},{7,23},{8,24},{9,... | collective-permute-start | bytes 909320 | tf_op jit(solution)/shard_map/ppermute | solution.py:697
  46.7 13.1 %collective-permute-start.13 = (bf16[1216,128]{1,0:T(8,128)(2,1)S(1)}, bf16[1216,128]{1,0:T(8,128)(2,1)S(1)}, u32[]{:S(2)}, u32[]{:S(2)}) collective-permute-start(bf16[1216,128]{1,0:T(8,128)(2,1)S(1)} %reduce-precision_convert_fusion.6), channel_id=1, source_target_pairs={{0,16},{1,17},{2,18},{3,19},{4,20},{5,21},{6,22},{7,23},{8,10},{9,... | collective-permute-start | bytes 933896 | tf_op jit(solution)/shard_map/ppermute | solution.py:697
  49.9 6.2 %collective-permute-start.10 = (bf16[608,128]{1,0:T(8,128)(2,1)S(1)}, bf16[608,128]{1,0:T(8,128)(2,1)S(1)}, u32[]{:S(2)}, u32[]{:S(2)}) collective-permute-start(bf16[608,128]{1,0:T(8,128)(2,1)S(1)} %slice.149), channel_id=1, source_target_pairs={{0,1},{1,0},{2,3},{3,2},{4,5},{5,4},{6,7},{7,6},{8,24},{9,25},{10,... | collective-permute-start | bytes 466952 | tf_op jit(solution)/shard_map/ppermute | solution.py:697
  52.4 27.3 %collective-permute-start.22 = (bf16[2,288,128]{2,1,0:T(8,128)(2,1)S(1)}, bf16[2,288,128]{2,1,0:T(8,128)(2,1)S(1)}, u32[]{:S(2)}, u32[]{:S(2)}) collective-permute-start(bf16[2,288,128]{2,1,0:T(8,128)(2,1)S(1)} %get-tuple-element.181), channel_id=1, source_target_pairs={{0,8},{1,9},{2,10},{3,11},{4,12},{5,13},{6,14},{7,15},{8,0},{9,1},... | collective-permute-start | bytes 442376 | tf_op jit(solution)/shard_map/ppermute | solution.py:697
  52.9 12.0 %collective-permute-start.9 = (bf16[592,128]{1,0:T(8,128)(2,1)S(1)}, bf16[592,128]{1,0:T(8,128)(2,1)S(1)}, u32[]{:S(2)}, u32[]{:S(2)}) collective-permute-start(bf16[592,128]{1,0:T(8,128)(2,1)S(1)} %reduce-precision_convert_fusion.15), channel_id=1, source_target_pairs={{0,4},{1,5},{2,6},{3,7},{4,0},{5,1},{6,2},{7,3},{8,12},{9,13},{10,... | collective-permute-start | bytes 454664 | tf_op jit(solution)/shard_map/ppermute | solution.py:697
  56.1 6.1 %collective-permute-start.11 = (bf16[304,128]{1,0:T(8,128)(2,1)S(1)}, bf16[304,128]{1,0:T(8,128)(2,1)S(1)}, u32[]{:S(2)}, u32[]{:S(2)}) collective-permute-start(bf16[304,128]{1,0:T(8,128)(2,1)S(1)} %slice.152), channel_id=1, source_target_pairs={{0,2},{1,3},{2,0},{3,1},{4,6},{5,7},{6,4},{7,5},{8,9},{9,8},{10,11... | collective-permute-start | bytes 233480 | tf_op jit(solution)/shard_map/ppermute | solution.py:697
  59.9 9.2 %collective-permute-start.16 = (bf16[608,128]{1,0:T(8,128)(2,1)S(1)}, bf16[608,128]{1,0:T(8,128)(2,1)S(1)}, u32[]{:S(2)}, u32[]{:S(2)}) collective-permute-start(bf16[608,128]{1,0:T(8,128)(2,1)S(1)} %slice.154), channel_id=1, source_target_pairs={{0,1},{1,0},{2,3},{3,2},{4,5},{5,4},{6,7},{7,6},{8,24},{9,25},{10,... | collective-permute-start | bytes 466952 | tf_op jit(solution)/shard_map/ppermute | solution.py:697
  60.5 5.9 %collective-permute-start.17 = (bf16[592,128]{1,0:T(8,128)(2,1)S(1)}, bf16[592,128]{1,0:T(8,128)(2,1)S(1)}, u32[]{:S(2)}, u32[]{:S(2)}) collective-permute-start(bf16[592,128]{1,0:T(8,128)(2,1)S(1)} %slice.155), channel_id=1, source_target_pairs={{0,2},{1,3},{2,0},{3,1},{4,6},{5,7},{6,4},{7,5},{8,9},{9,8},{10,11... | collective-permute-start | bytes 454664 | tf_op jit(solution)/shard_map/ppermute | solution.py:697
  62.2 9.5 %collective-permute-start.15 = (bf16[304,128]{1,0:T(8,128)(2,1)S(1)}, bf16[304,128]{1,0:T(8,128)(2,1)S(1)}, u32[]{:S(2)}, u32[]{:S(2)}) collective-permute-start(bf16[304,128]{1,0:T(8,128)(2,1)S(1)} %reduce-precision_convert_fusion.19), channel_id=1, source_target_pairs={{0,4},{1,5},{2,6},{3,7},{4,0},{5,1},{6,2},{7,3},{8,12},{9,13},{10,... | collective-permute-start | bytes 233480 | tf_op jit(solution)/shard_map/ppermute | solution.py:697
  65.0 6.9 %collective-permute-start.14 = (bf16[592,128]{1,0:T(8,128)(2,1)S(1)}, bf16[592,128]{1,0:T(8,128)(2,1)S(1)}, u32[]{:S(2)}, u32[]{:S(2)}) collective-permute-start(bf16[592,128]{1,0:T(8,128)(2,1)S(1)} %reduce-precision_convert_fusion.14), channel_id=1, source_target_pairs={{0,2},{1,3},{2,0},{3,1},{4,6},{5,7},{6,4},{7,5},{8,9},{9,8},{10,11... | collective-permute-start | bytes 454664 | tf_op jit(solution)/shard_map/ppermute | solution.py:697
  66.5 11.7 %collective-permute-start.23 = (bf16[592,128]{1,0:T(8,128)(2,1)S(1)}, bf16[592,128]{1,0:T(8,128)(2,1)S(1)}, u32[]{:S(2)}, u32[]{:S(2)}) collective-permute-start(bf16[592,128]{1,0:T(8,128)(2,1)S(1)} %reduce-precision_convert_fusion.13), channel_id=1, source_target_pairs={{0,4},{1,5},{2,6},{3,7},{4,0},{5,1},{6,2},{7,3},{8,12},{9,13},{10,... | collective-permute-start | bytes 454664 | tf_op jit(solution)/shard_map/ppermute | solution.py:697
  69.2 7.1 %collective-permute-start.19 = (bf16[304,128]{1,0:T(8,128)(2,1)S(1)}, bf16[304,128]{1,0:T(8,128)(2,1)S(1)}, u32[]{:S(2)}, u32[]{:S(2)}) collective-permute-start(bf16[304,128]{1,0:T(8,128)(2,1)S(1)} %slice.158), channel_id=1, source_target_pairs={{0,2},{1,3},{2,0},{3,1},{4,6},{5,7},{6,4},{7,5},{8,9},{9,8},{10,11... | collective-permute-start | bytes 233480 | tf_op jit(solution)/shard_map/ppermute | solution.py:697
  71.8 9.6 %collective-permute-start.21 = (bf16[304,128]{1,0:T(8,128)(2,1)S(1)}, bf16[304,128]{1,0:T(8,128)(2,1)S(1)}, u32[]{:S(2)}, u32[]{:S(2)}) collective-permute-start(bf16[304,128]{1,0:T(8,128)(2,1)S(1)} %reduce-precision_convert_fusion.18), channel_id=1, source_target_pairs={{0,2},{1,3},{2,0},{3,1},{4,6},{5,7},{6,4},{7,5},{8,9},{9,8},{10,11... | collective-permute-start | bytes 233480 | tf_op jit(solution)/shard_map/ppermute | solution.py:697
  71.9 17.1 %collective-permute-start.18 = (bf16[1184,128]{1,0:T(8,128)(2,1)S(1)}, bf16[1184,128]{1,0:T(8,128)(2,1)S(1)}, u32[]{:S(2)}, u32[]{:S(2)}) collective-permute-start(bf16[1184,128]{1,0:T(8,128)(2,1)S(1)} %pad_maximum_fusion.4), channel_id=1, source_target_pairs={{0,1},{1,0},{2,3},{3,2},{4,5},{5,4},{6,7},{7,6},{8,10},{9,11},{10,... | collective-permute-start | bytes 909320 | tf_op jit(solution)/shard_map/ppermute | solution.py:697
  76.3 6.3 %collective-permute-start.20 = (bf16[304,128]{1,0:T(8,128)(2,1)S(1)}, bf16[304,128]{1,0:T(8,128)(2,1)S(1)}, u32[]{:S(2)}, u32[]{:S(2)}) collective-permute-start(bf16[304,128]{1,0:T(8,128)(2,1)S(1)} %reduce-precision_convert_fusion.17), channel_id=1, source_target_pairs={{0,4},{1,5},{2,6},{3,7},{4,0},{5,1},{6,2},{7,3},{8,12},{9,13},{10,... | collective-permute-start | bytes 233480 | tf_op jit(solution)/shard_map/ppermute | solution.py:697
  78.2 6.8 %collective-permute-start.26 = (bf16[592,128]{1,0:T(8,128)(2,1)S(1)}, bf16[592,128]{1,0:T(8,128)(2,1)S(1)}, u32[]{:S(2)}, u32[]{:S(2)}) collective-permute-start(bf16[592,128]{1,0:T(8,128)(2,1)S(1)} %reduce-precision_convert_fusion.12), channel_id=1, source_target_pairs={{0,2},{1,3},{2,0},{3,1},{4,6},{5,7},{6,4},{7,5},{8,9},{9,8},{10,11... | collective-permute-start | bytes 454664 | tf_op jit(solution)/shard_map/ppermute | solution.py:697
  79.8 9.2 %collective-permute-start.28 = (bf16[4,288,128]{2,1,0:T(8,128)(2,1)S(1)}, bf16[4,288,128]{2,1,0:T(8,128)(2,1)S(1)}, u32[]{:S(2)}, u32[]{:S(2)}) collective-permute-start(bf16[4,288,128]{2,1,0:T(8,128)(2,1)S(1)} %pad_maximum_fusion.6), channel_id=1, source_target_pairs={{0,16},{1,17},{2,18},{3,19},{4,20},{5,21},{6,22},{7,23},{8,24},{9,... | collective-permute-start | bytes 884744 | tf_op jit(solution)/shard_map/ppermute | solution.py:697
  81.4 7.6 %collective-permute-start.27 = (bf16[608,128]{1,0:T(8,128)(2,1)S(1)}, bf16[608,128]{1,0:T(8,128)(2,1)S(1)}, u32[]{:S(2)}, u32[]{:S(2)}) collective-permute-start(bf16[608,128]{1,0:T(8,128)(2,1)S(1)} %pad_maximum_fusion.7), channel_id=1, source_target_pairs={{0,1},{1,0},{2,3},{3,2},{4,5},{5,4},{6,7},{7,6},{8,10},{9,11},{10,... | collective-permute-start | bytes 466952 | tf_op jit(solution)/shard_map/ppermute | solution.py:697
  85.0 8.6 %collective-permute-start.29 = (bf16[1184,128]{1,0:T(8,128)(2,1)S(1)}, bf16[1184,128]{1,0:T(8,128)(2,1)S(1)}, u32[]{:S(2)}, u32[]{:S(2)}) collective-permute-start(bf16[1184,128]{1,0:T(8,128)(2,1)S(1)} %pad_maximum_fusion.5), channel_id=1, source_target_pairs={{0,1},{1,0},{2,3},{3,2},{4,5},{5,4},{6,7},{7,6},{8,10},{9,11},{10,... | collective-permute-start | bytes 909320 | tf_op jit(solution)/shard_map/ppermute | solution.py:697
  (11 other events, 55.6 us)
